TPU v7x, 32 devices: a whole 2x2x4 slice. The times are simulated.
32 devices in a mesh: group: 8 (over y, x, core), member: 4 (over z).
Axes of the slice: x: 2, y: 2, z: 4, core: 2. Of those that a mesh axis runs over, the one named last changes fastest.
Arguments:
- spectra: bfloat16 [1024, 8, 2048], P(('group', 'member'))
- partner: int32 [8], replicated, may hold values from 0 to 7, as said below
Outputs:
- correlations: bfloat16 [1024, 128, 128], P(('group', 'member'))
Inputs may be any that keep to these rules, and one draw needn't show every extreme that they name: partner is one round of a round-robin among the 8 groups: partner[partner[g]] == g and partner[g] != g for every g.
All inputs are finite; a program needn't handle non-finite values.
Results may differ from a plain program's by a relative error of at most 0.007.
Values may be sent and summed in bfloat16 or wider, within the bound.
No kernel may reach another device: no remote copies, remote signals or barrier semaphores. Data moves between devices by JAX's collectives and lax.ppermute only.
A program may use at most 192 MiB of HBM per device.

v0:
```python
import math

import jax
import jax.numpy as jnp
from jax import lax
from jax.sharding import PartitionSpec as P

LAGS = 128
HALF = 64


def band_matrix(freq_count):
    positions = jnp.arange(freq_count, dtype=jnp.int32)
    distance = jnp.abs(positions[:, None] - positions[None, :])
    band_ones = (distance <= HALF).astype(jnp.float32)
    counts = (
        jnp.minimum(positions + HALF, freq_count - 1) - jnp.maximum(positions - HALF, 0) + 1
    ).astype(jnp.float32)
    return (band_ones, counts)


def whiten(spectra):
    freq_count = spectra.shape[2] // 2
    window_count = spectra.shape[1]
    real_part = spectra[:, :, :freq_count].astype(jnp.float32)
    imag_part = spectra[:, :, freq_count:].astype(jnp.float32)
    power_sum = jnp.sum(real_part * real_part + imag_part * imag_part, axis=1)
    band_ones, counts = band_matrix(freq_count)
    smoothed = jnp.dot(power_sum, band_ones, precision=lax.Precision.HIGHEST)
    average = smoothed / (counts * window_count)
    inverse_amp = 1.0 / jnp.sqrt(average + 1e-05)
    factor = jnp.concatenate([inverse_amp, inverse_amp], axis=1)
    return (spectra.astype(jnp.float32) * factor[:, None, :]).astype(jnp.bfloat16)


def lag_matrix(freq_count, window_count):
    lag_values = jnp.arange(LAGS, dtype=jnp.int32) - LAGS // 2
    freq_values = jnp.arange(freq_count, dtype=jnp.int32)
    residue = jnp.mod(freq_values[:, None] * lag_values[None, :], 2 * freq_count)
    angles = jnp.pi * residue.astype(jnp.float32) / freq_count
    norm_factor = 1.0 / math.sqrt(window_count * freq_count)
    return jnp.concatenate(
        [jnp.cos(angles) * norm_factor, -jnp.sin(angles) * norm_factor], axis=0
    ).astype(jnp.bfloat16)


def correlate(own_rows, other_rows, lag_table):
    freq_count = own_rows.shape[2] // 2
    own_real = own_rows[:, :, :freq_count]
    own_imag = own_rows[:, :, freq_count:]
    left_real = jnp.concatenate([own_real, own_imag], axis=1)
    left_imag = jnp.concatenate([own_imag, -own_real], axis=1)
    right_part = jnp.concatenate(
        [other_rows[:, :, :freq_count], other_rows[:, :, freq_count:]], axis=1
    )
    cross_real = jnp.einsum(
        "awf,bwf->abf", left_real, right_part, preferred_element_type=jnp.float32
    )
    cross_imag = jnp.einsum(
        "awf,bwf->abf", left_imag, right_part, preferred_element_type=jnp.float32
    )
    cross = jnp.concatenate([cross_real, cross_imag], axis=2).astype(jnp.bfloat16)
    own_count = own_rows.shape[0]
    other_count = other_rows.shape[0]
    lagged = jnp.dot(
        cross.reshape(own_count * other_count, 2 * freq_count),
        lag_table,
        preferred_element_type=jnp.float32,
    )
    return lagged.reshape(own_count, other_count, lag_table.shape[1])


def correlate_blocks(own_rows, other_rows, lag_table):
    row_count = other_rows.shape[0]
    block_size = math.gcd(row_count, max(1, 2048 // own_rows.shape[0]))
    stacked = other_rows.reshape((row_count // block_size, block_size) + other_rows.shape[1:])
    blocks_out = lax.map(lambda portion: correlate(own_rows, portion, lag_table), stacked)
    return jnp.transpose(blocks_out, (1, 0, 2, 3)).reshape(
        own_rows.shape[0], row_count, lag_table.shape[1]
    )


def on_device(spectra, partner):
    whitened = whiten(spectra)
    group_count = lax.axis_size("group")
    row_count = whitened.shape[0]
    spread = lax.all_to_all(whitened, "group", split_axis=0, concat_axis=0, tiled=True)
    blocks = spread.reshape((group_count, row_count // group_count) + whitened.shape[1:])
    ordered = jnp.take(blocks, partner, axis=0).reshape(whitened.shape)
    arrived = lax.all_to_all(ordered, "group", split_axis=0, concat_axis=0, tiled=True)
    lag_table = lag_matrix(whitened.shape[2] // 2, whitened.shape[1])
    theirs = lax.all_gather(arrived, "member", axis=0, tiled=True)
    result = correlate_blocks(whitened, theirs, lag_table)
    return result.astype(jnp.bfloat16)


def solution(mesh):
    placed = (P(("group", "member"), None, None), P())
    return jax.shard_map(
        on_device,
        mesh=mesh,
        in_specs=placed,
        out_specs=P(("group", "member"), None, None),
        check_vma=False,
    )
```

profile of v0, /device:TPU:0, one launch (start us, length us, event | category | flops | bytes accessed | tf_op | source)
XLA Modules:
  0.0 236.0 jit_solution(18232454043434663792)
XLA Ops:
  6.5 0.0 copy-start.1
  6.5 1.7 add_reduce_fusion
  8.3 0.0 copy-start.3
  8.3 0.7 fusion.15
  9.0 0.0 copy-done.1
  9.1 1.2 multiply_convert_fusion
  10.3 5.2 %all-to-all-start = ((bf16[32,8,2048]{2,1,0:T(8,128)(2,1)}), bf16[32,8,2048]{2,1,0:T(8,128)(2,1)S(1)}, u32[]{:S(2)}, u32[]{:S(2)}) async-start(bf16[32,8,2048]{2,1,0:T(8,128)(2,1)} %multiply_convert_fusion), calls=%async_computation | async-start | bytes 2097152 | tf_op jit(solution)/shard_map/all_to_all | solution.py:87
  15.5 0.0 all-gather.2.cloned.1.call-start
  15.5 0.0 copy-done.3
  15.5 0.1 broadcast_in_dim.28
  15.6 0.1 broadcast_in_dim.29
  15.7 15.2 %all-to-all-done = bf16[32,8,2048]{2,1,0:T(8,128)(2,1)S(1)} async-done(((bf16[32,8,2048]{2,1,0:T(8,128)(2,1)}), bf16[32,8,2048]{2,1,0:T(8,128)(2,1)S(1)}, u32[]{:S(2)}, u32[]{:S(2)}) %all-to-all-start) | async-done | bytes 1048608 | tf_op jit(solution)/shard_map/all_to_all | solution.py:87
  30.9 0.6 gather_fusion
  31.5 0.2 bitcast_select_fusion
  31.7 18.5 %all_to_all.10 = bf16[32,8,2048]{2,1,0:T(8,128)(2,1)} all-to-all(bf16[32,8,2048]{2,1,0:T(8,128)(2,1)S(1)} %bitcast_select_fusion), channel_id=1, replica_groups=mesh['group'=8,'member'=4] {'group'}, dimensions={0} | all-to-all | bytes 2097152 | tf_op jit(solution)/shard_map/all_to_all | solution.py:90
  50.2 0.0 all-gather.2.cloned.1.call-update
  50.2 1.3 slice_negate_fusion
  51.5 0.2 pad_maximum_fusion.5
  51.8 5.1 %copy.12 = bf16[32,16,1024]{0,1,2:T(8,128)(2,1)} copy(bf16[32,16,1024]{2,1,0:T(8,128)(2,1)S(1)} %get-tuple-element.103) | data formatting | bytes 2097152 | tf_op jit(solution)/shard_map/while | solution.py:77
  56.9 5.1 %copy.13 = bf16[32,16,1024]{0,1,2:T(8,128)(2,1)} copy(bf16[32,16,1024]{2,1,0:T(8,128)(2,1)S(1)} %get-tuple-element.102) | data formatting | bytes 2097152 | tf_op jit(solution)/shard_map/while | solution.py:77
  62.1 2.2 multiply_convert_fusion.2
  64.3 0.8 pad_maximum_fusion.6
  65.1 65.4 %all-gather.2.cloned.1.call-done = bf16[128,8,2048]{2,1,0:T(8,128)(2,1)} async-done(((bf16[32,8,2048]{2,1,0:T(8,128)(2,1)}), bf16[128,8,2048]{2,1,0:T(8,128)(2,1)}) %all-gather.2.cloned.1.call-update) | async-done | bytes 4194320 | tf_op jit(solution)/shard_map/all_gather | solution.py:92
  130.5 97.6 %while.12 = (s32[]{:T(128)}, bf16[2,32,64,128]{3,2,1,0:T(8,128)(2,1)S(1)}, bf16[2,64,8,2048]{3,2,1,0:T(8,128)(2,1)}, bf16[32,16,1024]{0,1,2:T(8,128)(2,1)}, bf16...) while((s32[]{:T(128)}, bf16[2,32,64,128]{3,2,1,0:T(8,128)(2,1)S(1)}, ...), condition=%wide.region_2.3_spmd, body=%wide.region_1.2_spmd.sunk | while | flops 1224736768 | bytes 60293260 | solution.py:77
  130.5 1.7 constant_dynamic-slice_fusion.2
  132.2 5.1 %copy.25 = bf16[1,64,8,2048]{1,2,3,0:T(8,128)(2,1)} copy(bf16[1,64,8,2048]{3,2,1,0:T(8,128)(2,1)S(1)} %constant_dynamic-slice_fusion.2) | data formatting | bytes 4194304 | tf_op jit(solution)/shard_map/while/body/jit(dynamic_index_in_dim)/dynamic_slice | solution.py:77
  137.4 0.0 copy-start
  137.4 2.6 %fusion.43 = (bf16[64,8,1024]{0,1,2:T(8,128)(2,1)S(1)}, bf16[64,8,1024]{0,1,2:T(8,128)(2,1)S(1)}) fusion(bf16[64,8,2048]{0,1,2:T(8,128)(2,1)} %bitcast.37), kind=kLoop, calls=%fused_computation.52.clone.1 | loop fusion | bytes 4194304 | tf_op jit(solution)/shard_map/while/body/eval_jaxpr/slice | solution.py:54
  140.0 0.8 copy-done
  140.8 3.1 %convert_bitcast_fusion.6 = bf16[32,64,1024]{1,0,2:T(8,128)(2,1)S(1)} fusion(bf16[32,16,1024]{0,1,2:T(8,128)(2,1)S(1)} %copy-done, bf16[64,8,1024]{0,1,2:T(8,128)(2,1)S(1)} %get-tuple-element.145, bf16[64,8,1024]{0,1,2:T(8,128)(2,1)S(1)} %get-tuple-element.146), kind=kOutput, calls=%fused_computation.5.clone.1 | convolution fusion | flops 73400320 | bytes 7340032 | tf_op jit(solution)/shard_map/while/body/eval_jaxpr/awf,bwf->abf/dot_general | solution.py:56
  144.0 4.5 %convert_bitcast_fusion.5 = bf16[32,64,1024]{1,0,2:T(8,128)(2,1)S(1)} fusion(bf16[32,16,1024]{0,1,2:T(8,128)(2,1)} %get-tuple-element.165, bf16[64,8,1024]{0,1,2:T(8,128)(2,1)S(1)} %get-tuple-element.145, bf16[64,8,1024]{0,1,2:T(8,128)(2,1)S(1)} %get-tuple-element.146), kind=kOutput, calls=%fused_computation.4.clone.1 | convolution fusion | flops 73400320 | bytes 7340032 | tf_op jit(solution)/shard_map/while/body/eval_jaxpr/awf,bwf->abf/dot_general | solution.py:59
  148.4 0.0 copy-start.2
  148.5 16.1 %pad_maximum_fusion.13 = bf16[32,64,2048]{1,0,2:T(8,128)(2,1)} fusion(bf16[32,64,1024]{1,0,2:T(8,128)(2,1)S(1)} %convert_bitcast_fusion.5, bf16[32,64,1024]{1,0,2:T(8,128)(2,1)S(1)} %convert_bitcast_fusion.6), kind=kLoop, calls=%fused_computation.1.clone.1 | loop fusion | flops 4194304 | bytes 16777216 | tf_op jit(solution)/shard_map/while/body/eval_jaxpr/concatenate | solution.py:62
  164.5 0.0 copy-done.2
  164.5 14.7 %fusion.44 = bf16[2,32,64,128]{3,2,1,0:T(8,128)(2,1)S(1)} fusion(bf16[2,32,64,128]{3,2,1,0:T(8,128)(2,1)S(1)} %get-tuple-element.155, s32[]{:T(128)} %get-tuple-element.154, bf16[32,64,2048]{1,0,2:T(8,128)(2,1)} %pad_maximum_fusion.13, bf16[2048,128]{1,0:T(8,128)(2,1)S(1)} %copy-done.2), kind=kOutput, calls=%fused_computation.8.clone.1 | convolution fusion | flops 1073741824 | bytes 9961476 | tf_op jit(solution)/shard_map/while/body/eval_jaxpr/dot_general | solution.py:65
  179.3 1.7 constant_dynamic-slice_fusion.2
  181.0 5.1 %copy.25 = bf16[1,64,8,2048]{1,2,3,0:T(8,128)(2,1)} copy(bf16[1,64,8,2048]{3,2,1,0:T(8,128)(2,1)S(1)} %constant_dynamic-slice_fusion.2) | data formatting | bytes 4194304 | tf_op jit(solution)/shard_map/while/body/jit(dynamic_index_in_dim)/dynamic_slice | solution.py:77
  186.2 0.0 copy-start
  186.2 2.6 %fusion.43 = (bf16[64,8,1024]{0,1,2:T(8,128)(2,1)S(1)}, bf16[64,8,1024]{0,1,2:T(8,128)(2,1)S(1)}) fusion(bf16[64,8,2048]{0,1,2:T(8,128)(2,1)} %bitcast.37), kind=kLoop, calls=%fused_computation.52.clone.1 | loop fusion | bytes 4194304 | tf_op jit(solution)/shard_map/while/body/eval_jaxpr/slice | solution.py:54
  188.8 0.8 copy-done
  189.6 3.1 %convert_bitcast_fusion.6 = bf16[32,64,1024]{1,0,2:T(8,128)(2,1)S(1)} fusion(bf16[32,16,1024]{0,1,2:T(8,128)(2,1)S(1)} %copy-done, bf16[64,8,1024]{0,1,2:T(8,128)(2,1)S(1)} %get-tuple-element.145, bf16[64,8,1024]{0,1,2:T(8,128)(2,1)S(1)} %get-tuple-element.146), kind=kOutput, calls=%fused_computation.5.clone.1 | convolution fusion | flops 73400320 | bytes 7340032 | tf_op jit(solution)/shard_map/while/body/eval_jaxpr/awf,bwf->abf/dot_general | solution.py:56
  192.8 4.5 %convert_bitcast_fusion.5 = bf16[32,64,1024]{1,0,2:T(8,128)(2,1)S(1)} fusion(bf16[32,16,1024]{0,1,2:T(8,128)(2,1)} %get-tuple-element.165, bf16[64,8,1024]{0,1,2:T(8,128)(2,1)S(1)} %get-tuple-element.145, bf16[64,8,1024]{0,1,2:T(8,128)(2,1)S(1)} %get-tuple-element.146), kind=kOutput, calls=%fused_computation.4.clone.1 | convolution fusion | flops 73400320 | bytes 7340032 | tf_op jit(solution)/shard_map/while/body/eval_jaxpr/awf,bwf->abf/dot_general | solution.py:59
  197.2 0.0 copy-start.2
  197.2 16.1 %pad_maximum_fusion.13 = bf16[32,64,2048]{1,0,2:T(8,128)(2,1)} fusion(bf16[32,64,1024]{1,0,2:T(8,128)(2,1)S(1)} %convert_bitcast_fusion.5, bf16[32,64,1024]{1,0,2:T(8,128)(2,1)S(1)} %convert_bitcast_fusion.6), kind=kLoop, calls=%fused_computation.1.clone.1 | loop fusion | flops 4194304 | bytes 16777216 | tf_op jit(solution)/shard_map/while/body/eval_jaxpr/concatenate | solution.py:62
  213.3 0.0 copy-done.2
  213.3 14.7 %fusion.44 = bf16[2,32,64,128]{3,2,1,0:T(8,128)(2,1)S(1)} fusion(bf16[2,32,64,128]{3,2,1,0:T(8,128)(2,1)S(1)} %get-tuple-element.155, s32[]{:T(128)} %get-tuple-element.154, bf16[32,64,2048]{1,0,2:T(8,128)(2,1)} %pad_maximum_fusion.13, bf16[2048,128]{1,0:T(8,128)(2,1)S(1)} %copy-done.2), kind=kOutput, calls=%fused_computation.8.clone.1 | convolution fusion | flops 1073741824 | bytes 9961476 | tf_op jit(solution)/shard_map/while/body/eval_jaxpr/dot_general | solution.py:65
  228.1 1.1 copy.14
  (7 shorter events, 0.1 us)
Async XLA Ops:
  6.5 2.5 %copy-start.1 = (bf16[32,8,2048]{2,1,0:T(8,128)(2,1)S(1)}, bf16[32,8,2048]{2,1,0:T(8,128)(2,1)}, u32[]{:S(2)}) copy-start(bf16[32,8,2048]{2,1,0:T(8,128)(2,1)} %param.4) | copy-start | bytes 3145732
  8.3 7.3 %copy-start.3 = (s32[8]{0:T(128)S(1)}, s32[8]{0:T(128)}, u32[]{:S(2)}) copy-start(s32[8]{0:T(128)} %param.5) | copy-start | bytes 100
  10.3 20.6 %all-to-all-start = ((bf16[32,8,2048]{2,1,0:T(8,128)(2,1)}), bf16[32,8,2048]{2,1,0:T(8,128)(2,1)S(1)}, u32[]{:S(2)}, u32[]{:S(2)}) async-start(bf16[32,8,2048]{2,1,0:T(8,128)(2,1)} %multiply_convert_fusion), calls=%async_computation | async-start | bytes 2097152 | tf_op jit(solution)/shard_map/all_to_all | solution.py:87
  15.5 115.0 %all-gather.2.cloned.1.call-start = ((), (), s32[]{:S(2)}) async-start(), calls=%async_computation.2 | async-start | bytes 5242880 | tf_op jit(solution)/shard_map/all_gather | solution.py:92
  137.4 3.4 %copy-start = (bf16[32,16,1024]{0,1,2:T(8,128)(2,1)S(1)}, bf16[32,16,1024]{0,1,2:T(8,128)(2,1)}, u32[]{:S(2)}) copy-start(bf16[32,16,1024]{0,1,2:T(8,128)(2,1)} %get-tuple-element.164) | copy-start | bytes 3145732 | tf_op jit(solution)/shard_map/while
  148.4 16.1 %copy-start.2 = (bf16[2048,128]{1,0:T(8,128)(2,1)S(1)}, bf16[2048,128]{1,0:T(8,128)(2,1)}, u32[]{:S(2)}) copy-start(bf16[2048,128]{1,0:T(8,128)(2,1)} %get-tuple-element.166) | copy-start | bytes 1572868 | tf_op jit(solution)/shard_map/while
  186.2 3.4 %copy-start = (bf16[32,16,1024]{0,1,2:T(8,128)(2,1)S(1)}, bf16[32,16,1024]{0,1,2:T(8,128)(2,1)}, u32[]{:S(2)}) copy-start(bf16[32,16,1024]{0,1,2:T(8,128)(2,1)} %get-tuple-element.164) | copy-start | bytes 3145732 | tf_op jit(solution)/shard_map/while
  197.2 16.1 %copy-start.2 = (bf16[2048,128]{1,0:T(8,128)(2,1)S(1)}, bf16[2048,128]{1,0:T(8,128)(2,1)}, u32[]{:S(2)}) copy-start(bf16[2048,128]{1,0:T(8,128)(2,1)} %get-tuple-element.166) | copy-start | bytes 1572868 | tf_op jit(solution)/shard_map/while
Sparse Core Ops, SparseCore 0:
  50.3 80.1 all-gather.1
where the time goes:
time: 236 us
  waiting for transfers between devices  80.6 us (34%)
  matrix products  45.4 us (19%)
  other arithmetic  39.9 us (17%)
  local copies, waits for them, and re-layouts  32.8 us (14%)
  blocking collectives  18.5 us (8%)
  between operations  13.5 us (6%)
  starting transfers between devices  5.21 us (2%)
    all_gather x1, waiting for transfers between devices, on_device(): theirs = lax.all_gather(arrived, 'member', axis=0, tiled=True)  65.4 us
    concatenate x2, other arithmetic, correlate(): jnp.concatenate([cross_real, cross_imag], axis=2).astype(jnp.bfloat16)  32.1 us
    dot_general x2, matrix products, correlate(): jnp.dot(cross.reshape(own_count * other_count, 2 * freq_count), lag_table...  29.5 us
    all_to_all x1, blocking collectives, on_device(): lax.all_to_all(ordered, 'group', split_axis=0, concat_axis=0, tiled=True)  18.5 us
    all_to_all x1, waiting for transfers between devices, on_device(): lax.all_to_all(whitened, 'group', split_axis=0, concat_axis=0, tiled=True)  15.2 us
    dynamic_slice x4, local copies, waits for them, and re-layouts, correlate_blocks(): lax.map(lambda portion: correlate(own_rows, portion, lag_table), stacked)  13.7 us
    while x2, local copies, waits for them, and re-layouts, correlate_blocks(): lax.map(lambda portion: correlate(own_rows, portion, lag_table), stacked)  10.3 us
    dot_general x2, matrix products, correlate(): jnp.einsum('awf,bwf->abf', left_imag, right_part, preferred_element_type=...  8.95 us
  transfers between devices with their start and end apart: 2, of which 2 were waited for; matrix products, arithmetic and copies ran while one was open for 6% of the time, Pallas kernels for 0%

commit v1 on v0

v1 whole, which is shorter than its diff:
```python
import itertools
import math

import jax
import jax.numpy as jnp
import ml_dtypes
import numpy as np
from jax import lax
from jax.experimental import pallas as pl
from jax.experimental.pallas import tpu as pltpu
from jax.sharding import PartitionSpec as P

LAGS = 128
HALF = 64
FINE = 16
ROWS = 16
VMEM_BYTES = 48 * 1024 * 1024


def lag_rows(freq_count, window_count):
    lag = np.arange(LAGS) - LAGS // 2
    freq = np.arange(freq_count)
    angle = np.pi * np.mod(lag[:, None] * freq[None, :], 2 * freq_count) / freq_count
    norm = 1.0 / math.sqrt(window_count * freq_count)
    rows = np.concatenate([np.cos(angle), -np.sin(angle)], axis=0) * norm
    return rows.astype(np.float32).astype(ml_dtypes.bfloat16)


def whiten_block(raw_ref, out_ref, wide_ref):
    rows, windows, width = raw_ref.shape
    freqs = width // 2
    lanes = windows * FINE
    groups = freqs // lanes
    for slab in range(2 * groups):
        value = raw_ref[:, :, slab * lanes : (slab + 1) * lanes].astype(jnp.float32)
        wide_ref[slab] = value.reshape(rows * windows, lanes)

    def window(slab, w):
        return wide_ref[slab, pl.ds(w, rows, stride=windows), :]

    pieces = []
    for group in range(groups):
        piece = jnp.zeros((rows, lanes), jnp.float32)
        for w in range(windows):
            real, imag = window(group, w), window(groups + group, w)
            piece += real * real + imag * imag
        pieces.append(piece)
    power = jnp.concatenate(pieces, axis=1)
    edge = jnp.zeros((rows, 2 * HALF), jnp.float32)
    padded = jnp.concatenate([edge, power, edge], axis=1)
    total = padded
    length = padded.shape[1]
    step = 1
    while step < 2 * HALF:
        total = total + pltpu.roll(total, length - step, axis=1)
        step *= 2
    total = total + pltpu.roll(padded, length - 2 * HALF, axis=1)
    smoothed = pltpu.roll(total, length - HALF, axis=1)[:, :freqs]
    place = lax.broadcasted_iota(jnp.int32, (rows, freqs), 1)
    counts = jnp.minimum(place + HALF, freqs - 1) - jnp.maximum(place - HALF, 0) + 1
    average = smoothed / (counts.astype(jnp.float32) * windows)
    factor = 1.0 / jnp.sqrt(average + 1e-05)
    granule = lax.broadcasted_iota(jnp.int32, (rows, lanes), 1) // FINE
    for part in range(2):
        for group in range(groups):
            scale = factor[:, group * lanes : (group + 1) * lanes]
            items = [window(part * groups + group, w) * scale for w in range(windows)]
            dist = windows // 2
            while dist:
                keep = (granule & dist) == 0
                nxt = list(items)
                for i in range(windows):
                    if i & dist:
                        continue
                    j = i + dist
                    nxt[i] = jnp.where(keep, items[i], pltpu.roll(items[j], dist * FINE, axis=1))
                    nxt[j] = jnp.where(keep, pltpu.roll(items[i], lanes - dist * FINE, axis=1), items[j])
                items = nxt
                dist //= 2
            for i in range(windows):
                out_ref[group * windows + i, :, part * lanes : (part + 1) * lanes] = items[i].astype(jnp.bfloat16)


def whiten(raw):
    channels, windows, width = raw.shape
    blocks = width // 2 // FINE
    return pl.pallas_call(
        whiten_block,
        grid=(channels // ROWS,),
        in_specs=[pl.BlockSpec((ROWS, windows, width), lambda i: (i, 0, 0))],
        out_specs=pl.BlockSpec((blocks, ROWS, 2 * windows * FINE), lambda i: (0, i, 0)),
        out_shape=jax.ShapeDtypeStruct((blocks, channels, 2 * windows * FINE), jnp.bfloat16),
        scratch_shapes=[pltpu.VMEM((blocks // windows * 2, ROWS * windows, windows * FINE), jnp.float32)],
        compiler_params=pltpu.CompilerParams(vmem_limit_bytes=VMEM_BYTES),
        name="whiten",
    )(raw)


def correlate_kernel(order_ref, a1, a2, b1, b2, b3, b4, table_ref, own_ref, other_ref, rows_ref, rhs_ref, cross_ref, flip_ref):
    step = pl.program_id(1)
    chunk, _, depth = a1.shape
    half = depth // 2
    a_count = 2 * ROWS
    b_count = 4 * ROWS
    width = 2 * b_count
    swap_a, swap_b, first_half = order_ref[0], order_ref[1], order_ref[2]
    fine_row = lax.broadcasted_iota(jnp.int32, (FINE, depth), 0)
    fine_lane = lax.broadcasted_iota(jnp.int32, (FINE, depth), 1) % FINE
    mask = (fine_row == fine_lane).astype(jnp.float32)

    def one_block(f, carry):
        for index, ref in enumerate((a1, a2)):
            at = pl.multiple_of((index ^ swap_a) * ROWS, ROWS)
            rows_ref[pl.ds(at, ROWS), :] = ref[f].astype(jnp.float32)
        for index, ref in enumerate((b1, b2, b3, b4)):
            spot = ((index // 2) ^ swap_b) * 2 + ((index % 2) ^ first_half)
            at = pl.multiple_of(spot * ROWS, ROWS)
            value = ref[f]
            rhs_ref[pl.ds(at, ROWS), :] = value
            rhs_ref[pl.ds(b_count + at, ROWS), :half] = -value[:, half:]
            rhs_ref[pl.ds(b_count + at, ROWS), half:] = value[:, :half]
        parts = []
        for i in range(a_count):
            row = jnp.broadcast_to(rows_ref[i : i + 1, :], (FINE, depth))
            parts.append((row * mask).astype(jnp.bfloat16))
        left = jnp.concatenate(parts, axis=0)
        cross = lax.dot_general(
            left, rhs_ref[...], (((1,), (1,)), ((), ())), preferred_element_type=jnp.float32
        ).astype(jnp.bfloat16)
        at = pl.multiple_of((step * chunk + f) * FINE, FINE)
        for i in range(a_count):
            cross_ref[pl.ds(at, FINE), i * width : (i + 1) * width] = cross[i * FINE : (i + 1) * FINE]
        return carry

    lax.fori_loop(0, chunk, one_block, 0)

    @pl.when(step == pl.num_programs(1) - 1)
    def _():
        low = lax.broadcasted_iota(jnp.int32, (LAGS, width), 1) < b_count
        for i in range(a_count):
            both = jnp.dot(
                table_ref[...], cross_ref[:, i * width : (i + 1) * width], preferred_element_type=jnp.float32
            )
            cos_part, sin_part = both[:LAGS], both[LAGS:]
            joined = jnp.where(
                low,
                cos_part + pltpu.roll(sin_part, b_count, axis=1),
                pltpu.roll(cos_part, b_count, axis=1) - sin_part,
            )
            turned = joined.T
            own_ref[(i // ROWS) ^ swap_a, i % ROWS] = turned[:b_count].astype(jnp.bfloat16)
            flip_ref[pl.ds(i, b_count, stride=a_count), :] = turned[b_count:]
        span = b_count // 2 * a_count
        for index in range(2):
            value = flip_ref[index * span : (index + 1) * span, :].astype(jnp.bfloat16)
            other_ref[index ^ swap_b] = value.reshape(b_count // 2, a_count, LAGS)


def correlate(order, a_list, b_list, table, b_blocks, chunk=8):
    blocks, _, depth = a_list[0][0].shape
    freqs = blocks * FINE
    a_count, b_count = 2 * ROWS, 4 * ROWS
    width = 2 * b_count
    stride = 4 if b_blocks > 1 else 0

    def spec(offset, advance):
        return pl.BlockSpec((chunk, ROWS, depth), lambda j, s, *_: (s, offset + advance * j, 0))

    return pl.pallas_call(
        correlate_kernel,
        grid_spec=pltpu.PrefetchScalarGridSpec(
            num_scalar_prefetch=1,
            grid=(b_blocks, blocks // chunk),
            in_specs=[spec(o, 0) for _, o in a_list]
            + [spec(o, stride) for _, o in b_list]
            + [pl.BlockSpec((2 * LAGS, freqs), lambda j, s, *_: (0, 0))],
            out_specs=[
                pl.BlockSpec((2, ROWS, b_count, LAGS), lambda j, s, *_: (0, 0, j, 0)),
                pl.BlockSpec((2, b_count // 2, a_count, LAGS), lambda j, s, *_: (0, j, 0, 0)),
            ],
            scratch_shapes=[
                pltpu.VMEM((a_count, depth), jnp.float32),
                pltpu.VMEM((width, depth), jnp.bfloat16),
                pltpu.VMEM((freqs, a_count * width), jnp.bfloat16),
                pltpu.VMEM((b_count * a_count, LAGS), jnp.float32),
            ],
        ),
        out_shape=[
            jax.ShapeDtypeStruct((2, ROWS, b_blocks * b_count, LAGS), jnp.bfloat16),
            jax.ShapeDtypeStruct((2, b_blocks * b_count // 2, a_count, LAGS), jnp.bfloat16),
        ],
        compiler_params=pltpu.CompilerParams(
            vmem_limit_bytes=VMEM_BYTES, dimension_semantics=("arbitrary", "arbitrary")
        ),
        name="correlate",
    )(order, *[a for a, _ in a_list], *[b for b, _ in b_list], table)


def whiten_half(raw, which):
    channels, windows, width = raw.shape
    blocks = width // 2 // FINE
    depth = 2 * windows * FINE

    def kernel(which_ref, raw_ref, out_ref, wide_ref):
        whiten_block(raw_ref, out_ref, wide_ref)

    return pl.pallas_call(
        kernel,
        grid_spec=pltpu.PrefetchScalarGridSpec(
            num_scalar_prefetch=1,
            grid=(1,),
            in_specs=[pl.BlockSpec((ROWS, windows, width), lambda i, which_ref: (which_ref[0], 0, 0))],
            out_specs=pl.BlockSpec((blocks, ROWS, depth), lambda i, *_: (0, 0, 0)),
            scratch_shapes=[pltpu.VMEM((blocks // windows * 2, ROWS * windows, windows * FINE), jnp.float32)],
        ),
        out_shape=jax.ShapeDtypeStruct((blocks, ROWS, depth), jnp.bfloat16),
        compiler_params=pltpu.CompilerParams(vmem_limit_bytes=VMEM_BYTES),
        name="whiten_half",
    )(which, raw)


def whiten_sorted(raw, own, stays):
    rows, windows, width = raw.shape
    blocks, _, depth = own.shape

    def kernel(stays_ref, raw_ref, own_ref, stay_ref, move_ref, new_ref, wide_ref):
        whiten_block(raw_ref, new_ref, wide_ref)

        @pl.when(stays_ref[0] == 1)
        def _():
            stay_ref[...] = own_ref[...]
            move_ref[...] = new_ref[...]

        @pl.when(stays_ref[0] != 1)
        def _():
            stay_ref[...] = new_ref[...]
            move_ref[...] = own_ref[...]

    shape = jax.ShapeDtypeStruct(own.shape, jnp.bfloat16)
    return pl.pallas_call(
        kernel,
        in_specs=[
            pl.BlockSpec(memory_space=pltpu.SMEM),
            pl.BlockSpec(memory_space=pltpu.VMEM),
            pl.BlockSpec(memory_space=pltpu.VMEM),
        ],
        out_specs=[pl.BlockSpec(memory_space=pltpu.VMEM)] * 2,
        out_shape=[shape, shape],
        scratch_shapes=[
            pltpu.VMEM(own.shape, jnp.bfloat16),
            pltpu.VMEM((blocks // windows * 2, ROWS * windows, windows * FINE), jnp.float32),
        ],
        compiler_params=pltpu.CompilerParams(vmem_limit_bytes=VMEM_BYTES),
        name="whiten_sorted",
    )(stays, raw, own)


def assign_roles(partner):
    count = partner.shape[0]
    chips = count // 2

    def kernel(partner_ref, out_ref):
        for group in range(count):
            out_ref[group] = -1
        for group in range(count):

            @pl.when(out_ref[group] < 0)
            def _():
                def walk(_, here):
                    there = partner_ref[here]
                    out_ref[here] = 0
                    out_ref[there] = 1
                    return there ^ 1

                lax.fori_loop(0, chips, walk, jnp.int32(group))

        target = [partner_ref[2 * chip + 1 - out_ref[2 * chip]] // 2 for chip in range(chips)]
        rank = jnp.int32(0)
        for i in range(chips):
            for j in range(i + 1, chips):
                rank += jnp.where(target[j] < target[i], math.factorial(chips - 1 - i), 0)
        out_ref[count] = rank

    return pl.pallas_call(
        kernel,
        in_specs=[pl.BlockSpec(memory_space=pltpu.SMEM)],
        out_specs=pl.BlockSpec(memory_space=pltpu.SMEM),
        out_shape=jax.ShapeDtypeStruct((count + 1,), jnp.int32),
        name="assign_roles",
    )(partner)


def permute(value, groups, members, target):
    pairs = []
    for group, member in itertools.product(range(groups), range(members)):
        to_group, to_member = target(group, member)
        pairs.append((group * members + member, to_group * members + to_member))
    return lax.ppermute(value, ("group", "member"), pairs)


def on_device_any(spectra, partner):
    group_count = lax.axis_size("group")
    channels, windows, width = spectra.shape
    white = whiten(spectra)
    blocks, _, depth = white.shape
    spread = lax.all_to_all(white, "group", split_axis=1, concat_axis=1, tiled=True)
    shares = spread.reshape(blocks, group_count, channels // group_count, depth)
    ordered = jnp.take(shares, partner, axis=1).reshape(white.shape)
    arrived = lax.all_to_all(ordered, "group", split_axis=1, concat_axis=1, tiled=True)
    theirs = lax.all_gather(arrived, "member", axis=1, tiled=True)
    table = jnp.asarray(lag_rows(width // 2, windows))
    others = theirs.shape[1]
    order = jnp.zeros((3,), jnp.int32)
    result, _ = correlate(
        order, [(white, 0), (white, 1)], [(theirs, q) for q in range(4)], table, others // (4 * ROWS)
    )
    return result.reshape(channels, others, LAGS)


def on_device_pairs(spectra, partner):
    groups, members = lax.axis_size("group"), lax.axis_size("member")
    chips = groups // 2
    channels, windows, width = spectra.shape
    group, member = lax.axis_index("group"), lax.axis_index("member")
    core = group % 2

    def across(value):
        return permute(value, groups, members, lambda g, m: (g ^ 1, m))

    roles = assign_roles(partner)
    rank = roles[groups]
    stays = 1 - lax.dynamic_slice_in_dim(roles, group, 1)
    received = across(lax.dynamic_slice_in_dim(spectra, (1 - core) * ROWS, ROWS, 0))
    own = whiten_half(spectra, core.reshape(1))
    stay, move = whiten_sorted(received, own, stays)

    far = (2, 0, 3, 1)
    back = tuple(far.index(m) for m in range(members))
    near = (0, 2, 1, 3)
    first = permute(stay, groups, members, lambda g, m: (g, far[m]))
    second = permute(stay, groups, members, lambda g, m: (g, near[m]))

    orders = list(itertools.permutations(range(chips)))

    def go(order):
        def branch(value):
            same = permute(value, groups, members, lambda g, m: (2 * order[g // 2] + g % 2, m))
            other = permute(value, groups, members, lambda g, m: (2 * order[g // 2] + g % 2, m ^ 1))
            return same, other

        return branch

    def home(order):
        def branch(same, other):
            same = permute(same, groups, members, lambda g, m: (2 * order.index(g // 2) + g % 2, m))
            other = permute(other, groups, members, lambda g, m: (2 * order.index(g // 2) + g % 2, m ^ 1))
            return same, other

        return branch

    here, there = lax.switch(rank, [go(order) for order in orders], move)
    table = jnp.asarray(lag_rows(width // 2, windows))
    order = jnp.stack([(member < 2).astype(jnp.int32), member % 2, core])
    straight, mirrored = correlate(
        order,
        [(first, 0), (second, 0)],
        [(here, 0), (across(here), 0), (there, 0), (across(there), 0)],
        table,
        1,
    )
    from_far = permute(straight[0], groups, members, lambda g, m: (g, back[m]))
    from_near = permute(straight[1], groups, members, lambda g, m: (g, near[m]))
    here, there = lax.switch(rank, [home(order) for order in orders], mirrored[0], mirrored[1])

    even = member % 2 == 0
    left, right = jnp.where(even, from_near, from_far), jnp.where(even, from_far, from_near)
    stay_part = jnp.concatenate([left, right], axis=1).reshape(-1, LAGS)
    left, right = jnp.where(even, here, there), jnp.where(even, there, here)
    move_part = jnp.concatenate([left, right], axis=1).reshape(-1, LAGS)
    stay_here = stays[0] == 1
    keep = jnp.where(stay_here, stay_part, move_part)
    got = across(jnp.where(stay_here, move_part, stay_part))
    low, high = jnp.where(core == 0, keep, got), jnp.where(core == 0, got, keep)
    others = channels * members
    as_stay = jnp.concatenate([low, high], axis=0).reshape(channels, others, LAGS)
    shape = (channels, members, 1, ROWS, LAGS)
    as_move = jnp.concatenate([low.reshape(shape), high.reshape(shape)], axis=2).reshape(channels, others, LAGS)
    return jnp.where(stay_here, as_stay, as_move)


def solution(mesh):
    placed = (P(("group", "member"), None, None), P())
    small = mesh.shape["group"] <= 8 and mesh.shape["member"] == 4
    return jax.shard_map(
        on_device_pairs if small else on_device_any,
        mesh=mesh,
        in_specs=placed,
        out_specs=P(("group", "member"), None, None),
        check_vma=False,
    )
```

time: 236 us -> 119 us (0.50)
  matrix products: 45.4 us -> 0 us
  waiting for transfers between devices: 80.6 us -> 38.8 us
  starting transfers between devices: 5.21 us -> 46.4 us
  other arithmetic: 39.9 us -> 2.88 us
  local copies, waits for them, and re-layouts: 32.8 us -> 1.85 us
  Pallas kernels: 0 us -> 27 us
  blocking collectives: 18.5 us -> 0 us
  between operations: 13.5 us -> 1.5 us
    all_gather x1 -> x0, waiting for transfers between devices: 65.4 us -> none  [on_device(): theirs = lax.all_gather(arrived, 'member', axis=0, tiled=True)]
    ppermute x0 -> x12, starting transfers between devices: none -> 46.4 us  [permute(): return lax.ppermute(value, ('group', 'member'), pairs)]
    dot_general x7 -> x0, matrix products: 45.4 us -> none  [the longest x2 29.5 us: correlate(): jnp.dot(cross.reshape(own_count * other_count, 2 * freq_count), lag_table...]
    ppermute x0 -> x12, waiting for transfers between devices: none -> 38.8 us  [permute(): return lax.ppermute(value, ('group', 'member'), pairs)]
    concatenate x5 -> x4, other arithmetic: 33.2 us -> 0.26 us  [the longest x1 0.09 us: on_device_pairs(): jnp.concatenate([low.reshape(shape), high.reshape(shape)], axis=2)]
    pallas_call x0 -> x4, Pallas kernels: none -> 27 us  [the longest x1 22.9 us: correlate(): pl.pallas_call(correlate_kernel, grid_spec=pltpu.PrefetchScalarGridSpec(n...]
    all_to_all x1 -> x0, blocking collectives: 18.5 us -> none  [on_device(): lax.all_to_all(ordered, 'group', split_axis=0, concat_axis=0, tiled=True)]
    all_to_all x1 -> x0, waiting for transfers between devices: 15.2 us -> none  [on_device(): lax.all_to_all(whitened, 'group', split_axis=0, concat_axis=0, tiled=True)]
  transfers between devices with their start and end apart: 2 -> 12, of which waited for: 2 -> 4; matrix products, arithmetic and copies ran while one was open for 6% -> 2% of each run, Pallas kernels for 0% -> 2%
where the time goes in v1:
time: 119 us; the launch traced here: 118 us
  starting transfers between devices  46.4 us (39%)
  waiting for transfers between devices  38.8 us (33%)
  Pallas kernels  27 us (23%)
  other arithmetic  2.88 us (2%)
  local copies, waits for them, and re-layouts  1.85 us (2%)
  between operations  1.5 us (1%)
    ppermute x12, starting transfers between devices, permute(): return lax.ppermute(value, ('group', 'member'), pairs)  46.4 us
    ppermute x12, waiting for transfers between devices, permute(): return lax.ppermute(value, ('group', 'member'), pairs)  38.8 us
    pallas_call x1, Pallas kernels, correlate(): pl.pallas_call(correlate_kernel, grid_spec=pltpu.PrefetchScalarGridSpec(n...  22.9 us
  transfers between devices with their start and end apart: 12, of which 4 were waited for; matrix products, arithmetic and copies ran while one was open for 2% of the time, Pallas kernels for 2%

profile of v1, /device:TPU:0, one launch (start us, length us, event | category | flops | bytes accessed | tf_op | source)
XLA Modules:
  0.0 118.5 jit_solution(15096636230741822)
XLA Ops:
  0.0 0.0 copy-start
  0.0 1.2 constant_dynamic-slice_fusion
  1.2 0.5 collective-permute-start.96
  1.7 1.3 %assign_roles.1 = s32[9]{0:T(128)} custom-call(s32[8]{0:T(128)} %partner_ref.1), custom_call_target="tpu_custom_call" | custom-call | tf_op jit(solution)/shard_map/assign_roles/pallas_call | solution.py:284
  3.0 0.0 copy-start.2
  3.0 0.0 copy-done
  3.0 0.0 copy-start.1
  3.0 1.4 %whiten_half.1.own_ref = bf16[64,16,256]{2,1,0:T(8,128)(2,1)S(1)} custom-call(s32[1]{0:T(128)} %bitcast.3.which_ref, bf16[32,8,2048]{2,1,0:T(8,128)(2,1)S(1)} %copy-done), custom_call_target="tpu_custom_call" | custom-call | tf_op jit(solution)/shard_map/whiten_half/pallas_call | solution.py:207
  4.4 0.0 copy-done.2
  4.4 0.6 fusion
  6.3 0.0 collective-permute-done.96.raw_ref
  6.3 1.4 %whiten_sorted.1 = (bf16[64,16,256]{2,1,0:T(8,128)(2,1)S(1)}, bf16[64,16,256]{2,1,0:T(8,128)(2,1)S(1)}) custom-call(s32[1]{0:T(128)S(6)} %sub.6.stays_ref, bf16[16,8,2048]{2,1,0:T(8,128)(2,1)S(1)} %collective-permute-done.96.raw_ref, bf16[64,16,256]{2,1,0:T(8,128)(2,1)S(1)} %whiten_half.1.own_ref), custom_call_target="tpu_custom_call" | custom-call | tf_op jit(solution)/shard_map/whiten_sorted/pallas_call | solution.py:240
  7.7 15.4 %conditional.2 = (bf16[64,16,256]{2,1,0:T(8,128)(2,1)}, bf16[64,16,256]{2,1,0:T(8,128)(2,1)}) conditional(s32[]{:T(128)} %bitcast.4, bf16[64,16,256]{2,1,0:T(8,128)(2,1)S(1)} %get-tuple-element.182, bf16[64,16,256]{2,1,0:T(8,128)(2,1)S(1)} %get-tuple-element.182, ...), branch_computations={%region_0.1_spmd, %region_1.2_spmd, %region_2.3_spmd, %region_3.4_... | conditional | bytes 4194400 | solution.py:361
  7.7 2.6 %collective-permute-start.7 = (bf16[64,16,256]{2,1,0:T(8,128)(2,1)S(1)}, bf16[64,16,256]{2,1,0:T(8,128)(2,1)}, u32[]{:S(2)}, u32[]{:S(2)}) collective-permute-start(bf16[64,16,256]{2,1,0:T(8,128)(2,1)S(1)} %param.3), channel_id=1, source_target_pairs={{0,1},{1,0},{2,3},{3,2},{4,5},{5,4},{6,7},{7,6},{8,17},{9,16},{10,... | collective-permute-start | bytes 1572872 | tf_op jit(solution)/shard_map/cond/branch_3_fun/ppermute | solution.py:298
  10.4 1.5 %collective-permute-start.6 = (bf16[64,16,256]{2,1,0:T(8,128)(2,1)S(1)}, bf16[64,16,256]{2,1,0:T(8,128)(2,1)}, u32[]{:S(2)}, u32[]{:S(2)}) collective-permute-start(bf16[64,16,256]{2,1,0:T(8,128)(2,1)S(1)} %param.3), channel_id=1, source_target_pairs={{0,0},{1,1},{2,2},{3,3},{4,4},{5,5},{6,6},{7,7},{8,16},{9,17},{10,... | collective-permute-start | bytes 1572872 | tf_op jit(solution)/shard_map/cond/branch_3_fun/ppermute | solution.py:298
  11.9 11.2 %collective-permute-done.7 = bf16[64,16,256]{2,1,0:T(8,128)(2,1)} collective-permute-done((bf16[64,16,256]{2,1,0:T(8,128)(2,1)S(1)}, bf16[64,16,256]{2,1,0:T(8,128)(2,1)}, u32[]{:S(2)}, u32[]{:S(2)}) %collective-permute-start.7) | collective-permute-done | bytes 524320 | tf_op jit(solution)/shard_map/cond/branch_3_fun/ppermute | solution.py:298
  23.1 0.0 collective-permute-done.6
  23.1 0.0 collective-permute-start.99
  23.1 18.0 %collective-permute-start.100 = (bf16[64,16,256]{2,1,0:T(8,128)(2,1)}, bf16[64,16,256]{2,1,0:T(8,128)(2,1)S(1)}, u32[]{:S(2)}, u32[]{:S(2)}) collective-permute-start(bf16[64,16,256]{2,1,0:T(8,128)(2,1)} %get-tuple-element.184.b3), channel_id=1, source_target_pairs={{0,4},{1,5},{2,6},{3,7},{4,0},{5,1},{6,2},{7,3},{8,12},{9,13},{10,... | collective-permute-start | bytes 1572872 | tf_op jit(solution)/shard_map/ppermute | solution.py:298
  41.1 0.7 collective-permute-start.98
  41.8 6.8 %collective-permute-start.97 = (bf16[64,16,256]{2,1,0:T(8,128)(2,1)S(1)}, bf16[64,16,256]{2,1,0:T(8,128)(2,1)S(1)}, u32[]{:S(2)}, u32[]{:S(2)}) collective-permute-start(bf16[64,16,256]{2,1,0:T(8,128)(2,1)S(1)} %get-tuple-element.181), channel_id=1, source_target_pairs={{0,2},{1,0},{2,3},{3,1},{4,6},{5,4},{6,7},{7,5},{8,10},{9,8},{10,1... | collective-permute-start | bytes 1572872 | tf_op jit(solution)/shard_map/ppermute | solution.py:298
  48.6 0.1 pad_add_fusion.order_ref
  48.7 0.0 collective-permute-done.99.b2
  48.7 0.0 collective-permute-done.100.b4
  48.7 0.0 collective-permute-done.98.a2
  48.7 13.8 %collective-permute-done.97.a1 = bf16[64,16,256]{2,1,0:T(8,128)(2,1)S(1)} collective-permute-done((bf16[64,16,256]{2,1,0:T(8,128)(2,1)S(1)}, bf16[64,16,256]{2,1,0:T(8,128)(2,1)S(1)}, u32[]{:S(2)}, u32[]{:S(2)}) %collective-permute-start.97) | collective-permute-done | bytes 524320 | tf_op jit(solution)/shard_map/ppermute | solution.py:298
  62.5 0.0 copy-done.1
  62.5 22.9 %correlate.1 = (bf16[2,16,64,128]{3,2,1,0:T(8,128)(2,1)S(1)}, bf16[2,32,32,128]{3,2,1,0:T(8,128)(2,1)S(1)}) custom-call(s32[3]{0:T(128)S(1)} %pad_add_fusion.order_ref, bf16[64,16,256]{2,1,0:T(8,128)(2,1)S(1)} %collective-permute-done.97.a1, bf16[64,16,256]{2,1,0:T(8,128)(2,1)S(1)} %collective-permute-done.98.a2, ...), custom_call_target="tpu_custom_call" | custom-call | tf_op jit(solution)/shard_map/correlate/pallas_call | solution.py:169
  85.5 0.7 collective-permute-start.101
  86.2 12.3 %collective-permute-start.102 = (bf16[16,64,128]{2,1,0:T(8,128)(2,1)S(1)}, bf16[16,64,128]{2,1,0:T(8,128)(2,1)S(1)}, u32[]{:S(2)}, u32[]{:S(2)}) collective-permute-start(bf16[16,64,128]{2,1,0:T(8,128)(2,1)S(1)} %get-tuple-element.194), channel_id=1, source_target_pairs={{0,1},{1,3},{2,0},{3,2},{4,5},{5,7},{6,4},{7,6},{8,9},{9,11},{10,8... | collective-permute-start | bytes 786440 | tf_op jit(solution)/shard_map/ppermute | solution.py:298
  98.5 15.1 %conditional.3 = (bf16[32,32,128]{2,1,0:T(8,128)(2,1)}, bf16[32,32,128]{2,1,0:T(8,128)(2,1)}) conditional(s32[]{:T(128)} %bitcast.4, (bf16[32,32,128]{2,1,0:T(8,128)(2,1)S(1)}, bf16[32,32,128]{2,1,0:T(8,128)(2,1)S(1)}) %tuple.197, (bf16[32,32,128]{2,1,0:T(8,128)(2,1)S(1)}, ...), branch_computations={%region_24.25_spmd, %region_25.26_spmd, %region_26.27_spmd, %regio... | conditional | bytes 2097248 | solution.py:373
  98.5 1.3 %collective-permute-start.54 = (bf16[32,32,128]{2,1,0:T(8,128)(2,1)S(1)}, bf16[32,32,128]{2,1,0:T(8,128)(2,1)}, u32[]{:S(2)}, u32[]{:S(2)}) collective-permute-start(bf16[32,32,128]{2,1,0:T(8,128)(2,1)S(1)} %get-tuple-element.131), channel_id=1, source_target_pairs={{0,0},{1,1},{2,2},{3,3},{4,4},{5,5},{6,6},{7,7},{8,24},{9,25},{10,... | collective-permute-start | bytes 786440 | tf_op jit(solution)/shard_map/cond/branch_3_fun/ppermute | solution.py:298
  99.9 1.9 %collective-permute-start.55 = (bf16[32,32,128]{2,1,0:T(8,128)(2,1)S(1)}, bf16[32,32,128]{2,1,0:T(8,128)(2,1)}, u32[]{:S(2)}, u32[]{:S(2)}) collective-permute-start(bf16[32,32,128]{2,1,0:T(8,128)(2,1)S(1)} %get-tuple-element.132), channel_id=1, source_target_pairs={{0,1},{1,0},{2,3},{3,2},{4,5},{5,4},{6,7},{7,6},{8,25},{9,24},{10,... | collective-permute-start | bytes 786440 | tf_op jit(solution)/shard_map/cond/branch_3_fun/ppermute | solution.py:298
  101.8 0.0 collective-permute-done.54
  101.8 11.8 %collective-permute-done.55 = bf16[32,32,128]{2,1,0:T(8,128)(2,1)} collective-permute-done((bf16[32,32,128]{2,1,0:T(8,128)(2,1)S(1)}, bf16[32,32,128]{2,1,0:T(8,128)(2,1)}, u32[]{:S(2)}, u32[]{:S(2)}) %collective-permute-start.55) | collective-permute-done | bytes 262176 | tf_op jit(solution)/shard_map/cond/branch_3_fun/ppermute | solution.py:298
  113.6 1.1 broadcast_select_fusion.3
  114.7 0.1 pad_maximum_fusion.3
  114.7 0.0 collective-permute-done.101
  114.7 0.0 collective-permute-done.102
  114.9 0.1 bitcast_select_fusion.1
  115.0 0.1 collective-permute-start.103
  115.1 1.9 %collective-permute-done.103 = bf16[2048,128]{1,0:T(8,128)(2,1)S(1)} collective-permute-done((bf16[2048,128]{1,0:T(8,128)(2,1)S(1)}, bf16[2048,128]{1,0:T(8,128)(2,1)S(1)}, u32[]{:S(2)}, u32[]{:S(2)}) %collective-permute-start.103) | collective-permute-done | bytes 524320 | tf_op jit(solution)/shard_map/ppermute | solution.py:298
  117.0 0.2 broadcast_select_fusion.1
  117.1 0.1 pad_maximum_fusion
  117.2 0.1 pad_maximum_fusion.1
  117.3 1.1 bitcast_select_fusion
  (4 shorter events, 0.1 us)
Async XLA Ops:
  0.0 3.0 %copy-start = (bf16[32,8,2048]{2,1,0:T(8,128)(2,1)S(1)}, bf16[32,8,2048]{2,1,0:T(8,128)(2,1)}, u32[]{:S(2)}) copy-start(bf16[32,8,2048]{2,1,0:T(8,128)(2,1)} %raw_ref.1) | copy-start | bytes 3145732
  1.2 5.1 %collective-permute-start.96 = (bf16[16,8,2048]{2,1,0:T(8,128)(2,1)S(1)}, bf16[16,8,2048]{2,1,0:T(8,128)(2,1)S(1)}, u32[]{:S(2)}, u32[]{:S(2)}) collective-permute-start(bf16[16,8,2048]{2,1,0:T(8,128)(2,1)S(1)} %constant_dynamic-slice_fusion), channel_id=1, source_target_pairs={{0,4},{1,5},{2,6},{3,7},{4,0},{5,1},{6,2},{7,3},{8,12},{9,13},{10,... | collective-permute-start | bytes 1572872 | tf_op jit(solution)/shard_map/ppermute | solution.py:298
  3.0 1.4 %copy-start.2 = (s32[9]{0:T(128)S(1)}, s32[9]{0:T(128)}, u32[]{:S(2)}) copy-start(s32[9]{0:T(128)} %assign_roles.1) | copy-start | bytes 112
  3.0 59.5 %copy-start.1 = (bf16[256,1024]{1,0:T(8,128)(2,1)S(1)}, bf16[256,1024]{1,0:T(8,128)(2,1)}, u32[]{:S(2)}) copy-start(bf16[256,1024]{1,0:T(8,128)(2,1)} %constant.46.clone.table_ref) | copy-start | bytes 1572868
  7.7 15.3 %collective-permute-start.7 = (bf16[64,16,256]{2,1,0:T(8,128)(2,1)S(1)}, bf16[64,16,256]{2,1,0:T(8,128)(2,1)}, u32[]{:S(2)}, u32[]{:S(2)}) collective-permute-start(bf16[64,16,256]{2,1,0:T(8,128)(2,1)S(1)} %param.3), channel_id=1, source_target_pairs={{0,1},{1,0},{2,3},{3,2},{4,5},{5,4},{6,7},{7,6},{8,17},{9,16},{10,... | collective-permute-start | bytes 1572872 | tf_op jit(solution)/shard_map/cond/branch_3_fun/ppermute | solution.py:298
  10.4 12.7 %collective-permute-start.6 = (bf16[64,16,256]{2,1,0:T(8,128)(2,1)S(1)}, bf16[64,16,256]{2,1,0:T(8,128)(2,1)}, u32[]{:S(2)}, u32[]{:S(2)}) collective-permute-start(bf16[64,16,256]{2,1,0:T(8,128)(2,1)S(1)} %param.3), channel_id=1, source_target_pairs={{0,0},{1,1},{2,2},{3,3},{4,4},{5,5},{6,6},{7,7},{8,16},{9,17},{10,... | collective-permute-start | bytes 1572872 | tf_op jit(solution)/shard_map/cond/branch_3_fun/ppermute | solution.py:298
  23.1 25.6 %collective-permute-start.99 = (bf16[64,16,256]{2,1,0:T(8,128)(2,1)}, bf16[64,16,256]{2,1,0:T(8,128)(2,1)S(1)}, u32[]{:S(2)}, u32[]{:S(2)}) collective-permute-start(bf16[64,16,256]{2,1,0:T(8,128)(2,1)} %get-tuple-element.183.b1), channel_id=1, source_target_pairs={{0,4},{1,5},{2,6},{3,7},{4,0},{5,1},{6,2},{7,3},{8,12},{9,13},{10,... | collective-permute-start | bytes 1572872 | tf_op jit(solution)/shard_map/ppermute | solution.py:298
  23.1 25.6 %collective-permute-start.100 = (bf16[64,16,256]{2,1,0:T(8,128)(2,1)}, bf16[64,16,256]{2,1,0:T(8,128)(2,1)S(1)}, u32[]{:S(2)}, u32[]{:S(2)}) collective-permute-start(bf16[64,16,256]{2,1,0:T(8,128)(2,1)} %get-tuple-element.184.b3), channel_id=1, source_target_pairs={{0,4},{1,5},{2,6},{3,7},{4,0},{5,1},{6,2},{7,3},{8,12},{9,13},{10,... | collective-permute-start | bytes 1572872 | tf_op jit(solution)/shard_map/ppermute | solution.py:298
  41.1 7.6 %collective-permute-start.98 = (bf16[64,16,256]{2,1,0:T(8,128)(2,1)S(1)}, bf16[64,16,256]{2,1,0:T(8,128)(2,1)S(1)}, u32[]{:S(2)}, u32[]{:S(2)}) collective-permute-start(bf16[64,16,256]{2,1,0:T(8,128)(2,1)S(1)} %get-tuple-element.181), channel_id=1, source_target_pairs={{0,0},{1,2},{2,1},{3,3},{4,4},{5,6},{6,5},{7,7},{8,8},{9,10},{10,9... | collective-permute-start | bytes 1572872 | tf_op jit(solution)/shard_map/ppermute | solution.py:298
  41.8 20.7 %collective-permute-start.97 = (bf16[64,16,256]{2,1,0:T(8,128)(2,1)S(1)}, bf16[64,16,256]{2,1,0:T(8,128)(2,1)S(1)}, u32[]{:S(2)}, u32[]{:S(2)}) collective-permute-start(bf16[64,16,256]{2,1,0:T(8,128)(2,1)S(1)} %get-tuple-element.181), channel_id=1, source_target_pairs={{0,2},{1,0},{2,3},{3,1},{4,6},{5,4},{6,7},{7,5},{8,10},{9,8},{10,1... | collective-permute-start | bytes 1572872 | tf_op jit(solution)/shard_map/ppermute | solution.py:298
  85.5 29.3 %collective-permute-start.101 = (bf16[16,64,128]{2,1,0:T(8,128)(2,1)S(1)}, bf16[16,64,128]{2,1,0:T(8,128)(2,1)S(1)}, u32[]{:S(2)}, u32[]{:S(2)}) collective-permute-start(bf16[16,64,128]{2,1,0:T(8,128)(2,1)S(1)} %get-tuple-element.193), channel_id=1, source_target_pairs={{0,0},{1,2},{2,1},{3,3},{4,4},{5,6},{6,5},{7,7},{8,8},{9,10},{10,9... | collective-permute-start | bytes 786440 | tf_op jit(solution)/shard_map/ppermute | solution.py:298
  86.2 28.6 %collective-permute-start.102 = (bf16[16,64,128]{2,1,0:T(8,128)(2,1)S(1)}, bf16[16,64,128]{2,1,0:T(8,128)(2,1)S(1)}, u32[]{:S(2)}, u32[]{:S(2)}) collective-permute-start(bf16[16,64,128]{2,1,0:T(8,128)(2,1)S(1)} %get-tuple-element.194), channel_id=1, source_target_pairs={{0,1},{1,3},{2,0},{3,2},{4,5},{5,7},{6,4},{7,6},{8,9},{9,11},{10,8... | collective-permute-start | bytes 786440 | tf_op jit(solution)/shard_map/ppermute | solution.py:298
  98.5 3.2 %collective-permute-start.54 = (bf16[32,32,128]{2,1,0:T(8,128)(2,1)S(1)}, bf16[32,32,128]{2,1,0:T(8,128)(2,1)}, u32[]{:S(2)}, u32[]{:S(2)}) collective-permute-start(bf16[32,32,128]{2,1,0:T(8,128)(2,1)S(1)} %get-tuple-element.131), channel_id=1, source_target_pairs={{0,0},{1,1},{2,2},{3,3},{4,4},{5,5},{6,6},{7,7},{8,24},{9,25},{10,... | collective-permute-start | bytes 786440 | tf_op jit(solution)/shard_map/cond/branch_3_fun/ppermute | solution.py:298
  99.9 13.7 %collective-permute-start.55 = (bf16[32,32,128]{2,1,0:T(8,128)(2,1)S(1)}, bf16[32,32,128]{2,1,0:T(8,128)(2,1)}, u32[]{:S(2)}, u32[]{:S(2)}) collective-permute-start(bf16[32,32,128]{2,1,0:T(8,128)(2,1)S(1)} %get-tuple-element.132), channel_id=1, source_target_pairs={{0,1},{1,0},{2,3},{3,2},{4,5},{5,4},{6,7},{7,6},{8,25},{9,24},{10,... | collective-permute-start | bytes 786440 | tf_op jit(solution)/shard_map/cond/branch_3_fun/ppermute | solution.py:298
  115.0 2.0 %collective-permute-start.103 = (bf16[2048,128]{1,0:T(8,128)(2,1)S(1)}, bf16[2048,128]{1,0:T(8,128)(2,1)S(1)}, u32[]{:S(2)}, u32[]{:S(2)}) collective-permute-start(bf16[2048,128]{1,0:T(8,128)(2,1)S(1)} %bitcast_select_fusion.1), channel_id=1, source_target_pairs={{0,4},{1,5},{2,6},{3,7},{4,0},{5,1},{6,2},{7,3},{8,12},{9,13},{10,... | collective-permute-start | bytes 1572872 | tf_op jit(solution)/shard_map/ppermute | solution.py:298

commit v2 on v1

--- a/solution.py
+++ b/solution.py
@@ -108,55 +108,56 @@
     fine_lane = lax.broadcasted_iota(jnp.int32, (FINE, depth), 1) % FINE
     mask = (fine_row == fine_lane).astype(jnp.float32)
 
-    def one_block(f, carry):
-        for index, ref in enumerate((a1, a2)):
-            at = pl.multiple_of((index ^ swap_a) * ROWS, ROWS)
-            rows_ref[pl.ds(at, ROWS), :] = ref[f].astype(jnp.float32)
-        for index, ref in enumerate((b1, b2, b3, b4)):
-            spot = ((index // 2) ^ swap_b) * 2 + ((index % 2) ^ first_half)
-            at = pl.multiple_of(spot * ROWS, ROWS)
+    for index, ref in enumerate((a1, a2)):
+        at = pl.multiple_of((index ^ swap_a) * ROWS, ROWS)
+        for f in range(chunk):
+            rows_ref[f, pl.ds(at, ROWS), :] = ref[f].astype(jnp.float32)
+    for index, ref in enumerate((b1, b2, b3, b4)):
+        spot = ((index // 2) ^ swap_b) * 2 + ((index % 2) ^ first_half)
+        at = pl.multiple_of(spot * ROWS, ROWS)
+        for f in range(chunk):
             value = ref[f]
-            rhs_ref[pl.ds(at, ROWS), :] = value
-            rhs_ref[pl.ds(b_count + at, ROWS), :half] = -value[:, half:]
-            rhs_ref[pl.ds(b_count + at, ROWS), half:] = value[:, :half]
+            rhs_ref[f, pl.ds(at, ROWS), :] = value
+            rhs_ref[f, pl.ds(b_count + at, ROWS), :half] = -value[:, half:]
+            rhs_ref[f, pl.ds(b_count + at, ROWS), half:] = value[:, :half]
+    for f in range(chunk):
         parts = []
         for i in range(a_count):
-            row = jnp.broadcast_to(rows_ref[i : i + 1, :], (FINE, depth))
+            row = jnp.broadcast_to(rows_ref[f, i : i + 1, :], (FINE, depth))
             parts.append((row * mask).astype(jnp.bfloat16))
         left = jnp.concatenate(parts, axis=0)
         cross = lax.dot_general(
-            left, rhs_ref[...], (((1,), (1,)), ((), ())), preferred_element_type=jnp.float32
+            left, rhs_ref[f], (((1,), (1,)), ((), ())), preferred_element_type=jnp.float32
         ).astype(jnp.bfloat16)
         at = pl.multiple_of((step * chunk + f) * FINE, FINE)
         for i in range(a_count):
             cross_ref[pl.ds(at, FINE), i * width : (i + 1) * width] = cross[i * FINE : (i + 1) * FINE]
-        return carry
-
-    lax.fori_loop(0, chunk, one_block, 0)
 
     @pl.when(step == pl.num_programs(1) - 1)
     def _():
         low = lax.broadcasted_iota(jnp.int32, (LAGS, width), 1) < b_count
-        for i in range(a_count):
-            both = jnp.dot(
-                table_ref[...], cross_ref[:, i * width : (i + 1) * width], preferred_element_type=jnp.float32
+        for pair in range(a_count // 2):
+            wide = jnp.dot(
+                table_ref[...], cross_ref[:, 2 * pair * width : 2 * (pair + 1) * width], preferred_element_type=jnp.float32
             )
-            cos_part, sin_part = both[:LAGS], both[LAGS:]
-            joined = jnp.where(
-                low,
-                cos_part + pltpu.roll(sin_part, b_count, axis=1),
-                pltpu.roll(cos_part, b_count, axis=1) - sin_part,
-            )
-            turned = joined.T
-            own_ref[(i // ROWS) ^ swap_a, i % ROWS] = turned[:b_count].astype(jnp.bfloat16)
-            flip_ref[pl.ds(i, b_count, stride=a_count), :] = turned[b_count:]
+            for i in (2 * pair, 2 * pair + 1):
+                both = wide[:, (i % 2) * width : (i % 2 + 1) * width]
+                cos_part, sin_part = both[:LAGS], both[LAGS:]
+                joined = jnp.where(
+                    low,
+                    cos_part + pltpu.roll(sin_part, b_count, axis=1),
+                    pltpu.roll(cos_part, b_count, axis=1) - sin_part,
+                )
+                turned = joined.T
+                own_ref[(i // ROWS) ^ swap_a, i % ROWS] = turned[:b_count].astype(jnp.bfloat16)
+                flip_ref[pl.ds(i, b_count, stride=a_count), :] = turned[b_count:]
         span = b_count // 2 * a_count
         for index in range(2):
             value = flip_ref[index * span : (index + 1) * span, :].astype(jnp.bfloat16)
             other_ref[index ^ swap_b] = value.reshape(b_count // 2, a_count, LAGS)
 
 
-def correlate(order, a_list, b_list, table, b_blocks, chunk=8):
+def correlate(order, a_list, b_list, table, b_blocks, chunk=16):
     blocks, _, depth = a_list[0][0].shape
     freqs = blocks * FINE
     a_count, b_count = 2 * ROWS, 4 * ROWS
@@ -179,8 +180,8 @@
                 pl.BlockSpec((2, b_count // 2, a_count, LAGS), lambda j, s, *_: (0, j, 0, 0)),
             ],
             scratch_shapes=[
-                pltpu.VMEM((a_count, depth), jnp.float32),
-                pltpu.VMEM((width, depth), jnp.bfloat16),
+                pltpu.VMEM((chunk, a_count, depth), jnp.float32),
+                pltpu.VMEM((chunk, width, depth), jnp.bfloat16),
                 pltpu.VMEM((freqs, a_count * width), jnp.bfloat16),
                 pltpu.VMEM((b_count * a_count, LAGS), jnp.float32),
             ],
@@ -337,28 +338,29 @@
     far = (2, 0, 3, 1)
     back = tuple(far.index(m) for m in range(members))
     near = (0, 2, 1, 3)
-    first = permute(stay, groups, members, lambda g, m: (g, far[m]))
-    second = permute(stay, groups, members, lambda g, m: (g, near[m]))
-
     orders = list(itertools.permutations(range(chips)))
 
     def go(order):
-        def branch(value):
-            same = permute(value, groups, members, lambda g, m: (2 * order[g // 2] + g % 2, m))
-            other = permute(value, groups, members, lambda g, m: (2 * order[g // 2] + g % 2, m ^ 1))
-            return same, other
+        def branch(stay, move):
+            first = permute(stay, groups, members, lambda g, m: (g, far[m]))
+            second = permute(stay, groups, members, lambda g, m: (g, near[m]))
+            same = permute(move, groups, members, lambda g, m: (2 * order[g // 2] + g % 2, m))
+            other = permute(move, groups, members, lambda g, m: (2 * order[g // 2] + g % 2, m ^ 1))
+            return first, second, same, other
 
         return branch
 
     def home(order):
-        def branch(same, other):
+        def branch(first, second, same, other):
+            first = permute(first, groups, members, lambda g, m: (g, back[m]))
+            second = permute(second, groups, members, lambda g, m: (g, near[m]))
             same = permute(same, groups, members, lambda g, m: (2 * order.index(g // 2) + g % 2, m))
             other = permute(other, groups, members, lambda g, m: (2 * order.index(g // 2) + g % 2, m ^ 1))
-            return same, other
+            return first, second, same, other
 
         return branch
 
-    here, there = lax.switch(rank, [go(order) for order in orders], move)
+    first, second, here, there = lax.switch(rank, [go(order) for order in orders], stay, move)
     table = jnp.asarray(lag_rows(width // 2, windows))
     order = jnp.stack([(member < 2).astype(jnp.int32), member % 2, core])
     straight, mirrored = correlate(
@@ -368,9 +370,9 @@
         table,
         1,
     )
-    from_far = permute(straight[0], groups, members, lambda g, m: (g, back[m]))
-    from_near = permute(straight[1], groups, members, lambda g, m: (g, near[m]))
-    here, there = lax.switch(rank, [home(order) for order in orders], mirrored[0], mirrored[1])
+    from_far, from_near, here, there = lax.switch(
+        rank, [home(order) for order in orders], straight[0], straight[1], mirrored[0], mirrored[1]
+    )
 
     even = member % 2 == 0
     left, right = jnp.where(even, from_near, from_far), jnp.where(even, from_far, from_near)

time: 119 us -> 86.1 us (0.72)
  the two profiles are of different devices: /device:TPU:0 before, /device:TPU:19 now
where the time goes in v2:
time: 86.1 us; the launch traced here: 84.5 us
  waiting for transfers between devices  38.5 us (45%)
  starting transfers between devices  23 us (27%)
  Pallas kernels  14.8 us (17%)
  other arithmetic  3.91 us (5%)
  local copies, waits for them, and re-layouts  2.65 us (3%)
  between operations  1.5 us (2%)
    ppermute x12, waiting for transfers between devices, permute(): return lax.ppermute(value, ('group', 'member'), pairs)  38.5 us
    ppermute x12, starting transfers between devices, permute(): return lax.ppermute(value, ('group', 'member'), pairs)  23 us
    pallas_call x1, Pallas kernels, correlate(): pl.pallas_call(correlate_kernel, grid_spec=pltpu.PrefetchScalarGridSpec(n...  10.7 us
  transfers between devices with their start and end apart: 12, of which 8 were waited for; matrix products, arithmetic and copies ran while one was open for 2% of the time, Pallas kernels for 3%

profile of v2, /device:TPU:19, one launch (start us, length us, event | category | flops | bytes accessed | tf_op | source)
XLA Modules:
  0.0 84.5 jit_solution(9053384985264943050)
XLA Ops:
  0.0 0.0 copy-start
  0.0 1.2 %constant_dynamic-slice_fusion = bf16[16,8,2048]{2,1,0:T(8,128)(2,1)S(1)} fusion(bf16[32,8,2048]{2,1,0:T(8,128)(2,1)} %raw_ref.1, s32[]{:T(128)S(6)} %select_n.80), kind=kLoop, calls=%fused_computation.18 | loop fusion | bytes 1048580 | tf_op jit(solution)/shard_map/dynamic_slice | solution.py:334
  1.2 0.7 collective-permute-start.192
  1.9 0.0 copy-done
  1.9 0.0 copy-start.1
  1.9 1.3 %whiten_half.1.own_ref = bf16[64,16,256]{2,1,0:T(8,128)(2,1)S(1)} custom-call(s32[1]{0:T(128)} %bitcast.4.which_ref, bf16[32,8,2048]{2,1,0:T(8,128)(2,1)S(1)} %copy-done), custom_call_target="tpu_custom_call" | custom-call | tf_op jit(solution)/shard_map/whiten_half/pallas_call | solution.py:208
  3.3 1.3 %assign_roles.1 = s32[9]{0:T(128)} custom-call(s32[8]{0:T(128)} %partner_ref.1), custom_call_target="tpu_custom_call" | custom-call | tf_op jit(solution)/shard_map/assign_roles/pallas_call | solution.py:285
  4.6 1.4 %fusion = (s32[1]{0:T(128)}, s32[1]{0:T(128)}) fusion(s32[9]{0:T(128)} %assign_roles.1, s32[]{:T(128)S(6)} %select_n.73), kind=kLoop, calls=%fused_computation.19 | loop fusion | bytes 20 | tf_op jit(solution)/shard_map/dynamic_slice | solution.py:333
  7.4 0.0 collective-permute-done.192.raw_ref
  7.4 1.4 %whiten_sorted.1 = (bf16[64,16,256]{2,1,0:T(8,128)(2,1)S(1)}, bf16[64,16,256]{2,1,0:T(8,128)(2,1)S(1)}) custom-call(s32[1]{0:T(128)S(6)} %sub.6.stays_ref, bf16[16,8,2048]{2,1,0:T(8,128)(2,1)S(1)} %collective-permute-done.192.raw_ref, bf16[64,16,256]{2,1,0:T(8,128)(2,1)S(1)} %whiten_half.1.own_ref), custom_call_target="tpu_custom_call" | custom-call | tf_op jit(solution)/shard_map/whiten_sorted/pallas_call | solution.py:241
  8.8 29.6 %conditional.2 = (bf16[64,16,256]{2,1,0:T(8,128)(2,1)}, bf16[64,16,256]{2,1,0:T(8,128)(2,1)}, bf16[64,16,256]{2,1,0:T(8,128)(2,1)}, bf16[64,16,256]{2,1,0:T(8,128)(2,1)}) conditional(s32[]{:T(128)} %bitcast.1, (bf16[64,16,256]{2,1,0:T(8,128)(2,1)S(1)}, bf16[64,16,256]{2,1,0:T(8,128)(2,1)S(1)}) %whiten_sorted.1, ...), branch_computations={%region_0.1_spmd, %region_1.2_spmd, %region_2.3_spmd, %region_3.4_... | conditional | bytes 8388800 | solution.py:363
  8.9 1.3 %collective-permute-start.12 = (bf16[64,16,256]{2,1,0:T(8,128)(2,1)S(1)}, bf16[64,16,256]{2,1,0:T(8,128)(2,1)}, u32[]{:S(2)}, u32[]{:S(2)}) collective-permute-start(bf16[64,16,256]{2,1,0:T(8,128)(2,1)S(1)} %get-tuple-element.299), channel_id=1, source_target_pairs={{0,2},{1,0},{2,3},{3,1},{4,6},{5,4},{6,7},{7,5},{8,10},{9,8},{10,1... | collective-permute-start | bytes 1572872 | tf_op jit(solution)/shard_map/cond/branch_3_fun/ppermute | solution.py:299
  10.2 1.9 %collective-permute-start.13 = (bf16[64,16,256]{2,1,0:T(8,128)(2,1)S(1)}, bf16[64,16,256]{2,1,0:T(8,128)(2,1)}, u32[]{:S(2)}, u32[]{:S(2)}) collective-permute-start(bf16[64,16,256]{2,1,0:T(8,128)(2,1)S(1)} %get-tuple-element.299), channel_id=1, source_target_pairs={{0,0},{1,2},{2,1},{3,3},{4,4},{5,6},{6,5},{7,7},{8,8},{9,10},{10,9... | collective-permute-start | bytes 1572872 | tf_op jit(solution)/shard_map/cond/branch_3_fun/ppermute | solution.py:299
  12.1 3.1 %collective-permute-start.14 = (bf16[64,16,256]{2,1,0:T(8,128)(2,1)S(1)}, bf16[64,16,256]{2,1,0:T(8,128)(2,1)}, u32[]{:S(2)}, u32[]{:S(2)}) collective-permute-start(bf16[64,16,256]{2,1,0:T(8,128)(2,1)S(1)} %get-tuple-element.300), channel_id=1, source_target_pairs={{0,0},{1,1},{2,2},{3,3},{4,4},{5,5},{6,6},{7,7},{8,16},{9,17},{10,... | collective-permute-start | bytes 1572872 | tf_op jit(solution)/shard_map/cond/branch_3_fun/ppermute | solution.py:299
  15.2 0.6 collective-permute-start.15
  15.8 7.5 %collective-permute-done.12 = bf16[64,16,256]{2,1,0:T(8,128)(2,1)} collective-permute-done((bf16[64,16,256]{2,1,0:T(8,128)(2,1)S(1)}, bf16[64,16,256]{2,1,0:T(8,128)(2,1)}, u32[]{:S(2)}, u32[]{:S(2)}) %collective-permute-start.12) | collective-permute-done | bytes 524320 | tf_op jit(solution)/shard_map/cond/branch_3_fun/ppermute | solution.py:299
  23.3 11.7 %collective-permute-done.13 = bf16[64,16,256]{2,1,0:T(8,128)(2,1)} collective-permute-done((bf16[64,16,256]{2,1,0:T(8,128)(2,1)S(1)}, bf16[64,16,256]{2,1,0:T(8,128)(2,1)}, u32[]{:S(2)}, u32[]{:S(2)}) %collective-permute-start.13) | collective-permute-done | bytes 524320 | tf_op jit(solution)/shard_map/cond/branch_3_fun/ppermute | solution.py:299
  35.0 3.4 %collective-permute-done.14 = bf16[64,16,256]{2,1,0:T(8,128)(2,1)} collective-permute-done((bf16[64,16,256]{2,1,0:T(8,128)(2,1)S(1)}, bf16[64,16,256]{2,1,0:T(8,128)(2,1)}, u32[]{:S(2)}, u32[]{:S(2)}) %collective-permute-start.14) | collective-permute-done | bytes 524320 | tf_op jit(solution)/shard_map/cond/branch_3_fun/ppermute | solution.py:299
  38.4 0.0 collective-permute-done.15
  38.4 1.3 %collective-permute-start.193 = (bf16[64,16,256]{2,1,0:T(8,128)(2,1)}, bf16[64,16,256]{2,1,0:T(8,128)(2,1)S(1)}, u32[]{:S(2)}, u32[]{:S(2)}) collective-permute-start(bf16[64,16,256]{2,1,0:T(8,128)(2,1)} %get-tuple-element.449.b1), channel_id=1, source_target_pairs={{0,4},{1,5},{2,6},{3,7},{4,0},{5,1},{6,2},{7,3},{8,12},{9,13},{10,... | collective-permute-start | bytes 1572872 | tf_op jit(solution)/shard_map/ppermute | solution.py:299
  39.7 4.8 %collective-permute-start.194 = (bf16[64,16,256]{2,1,0:T(8,128)(2,1)}, bf16[64,16,256]{2,1,0:T(8,128)(2,1)S(1)}, u32[]{:S(2)}, u32[]{:S(2)}) collective-permute-start(bf16[64,16,256]{2,1,0:T(8,128)(2,1)} %get-tuple-element.450.b3), channel_id=1, source_target_pairs={{0,4},{1,5},{2,6},{3,7},{4,0},{5,1},{6,2},{7,3},{8,12},{9,13},{10,... | collective-permute-start | bytes 1572872 | tf_op jit(solution)/shard_map/ppermute | solution.py:299
  44.5 0.1 pad_add_fusion.order_ref
  44.6 0.0 collective-permute-done.193.b2
  44.6 1.9 %collective-permute-done.194.b4 = bf16[64,16,256]{2,1,0:T(8,128)(2,1)S(1)} collective-permute-done((bf16[64,16,256]{2,1,0:T(8,128)(2,1)}, bf16[64,16,256]{2,1,0:T(8,128)(2,1)S(1)}, u32[]{:S(2)}, u32[]{:S(2)}) %collective-permute-start.194) | collective-permute-done | bytes 524320 | tf_op jit(solution)/shard_map/ppermute | solution.py:299
  46.5 0.0 copy-done.1
  46.5 10.7 %correlate.1 = (bf16[2,16,64,128]{3,2,1,0:T(8,128)(2,1)S(1)}, bf16[2,32,32,128]{3,2,1,0:T(8,128)(2,1)S(1)}) custom-call(s32[3]{0:T(128)S(1)} %pad_add_fusion.order_ref, bf16[64,16,256]{2,1,0:T(8,128)(2,1)} %get-tuple-element.447.a1, bf16[64,16,256]{2,1,0:T(8,128)(2,1)} %get-tuple-element.448.a2, bf16[64,16,256]{2,1,0:T(8,128)(2,1)} %get-tuple-element.449.b1, ...), custom_call_target="tpu_custom_call" | custom-call | tf_op jit(solution)/shard_map/correlate/pallas_call | solution.py:170
  57.3 20.1 %conditional.3 = (bf16[16,64,128]{2,1,0:T(8,128)(2,1)}, bf16[16,64,128]{2,1,0:T(8,128)(2,1)}, bf16[32,32,128]{2,1,0:T(8,128)(2,1)}, bf16[32,32,128]{2,1,0:T(8,128)(2,1)}) conditional(s32[]{:T(128)} %bitcast.1, (bf16[16,64,128]{2,1,0:T(8,128)(2,1)S(1)}, bf16[16,64,128]{2,1,0:T(8,128)(2,1)S(1)}, ...), branch_computations={%region_24.25_spmd, %region_25.26_spmd, %region_26.27_spmd, %regio... | conditional | bytes 4194496 | solution.py:373
  57.3 0.3 collective-permute-start.108
  57.7 4.0 %collective-permute-start.109 = (bf16[16,64,128]{2,1,0:T(8,128)(2,1)S(1)}, bf16[16,64,128]{2,1,0:T(8,128)(2,1)}, u32[]{:S(2)}, u32[]{:S(2)}) collective-permute-start(bf16[16,64,128]{2,1,0:T(8,128)(2,1)S(1)} %get-tuple-element.354), channel_id=1, source_target_pairs={{0,0},{1,2},{2,1},{3,3},{4,4},{5,6},{6,5},{7,7},{8,8},{9,10},{10,9... | collective-permute-start | bytes 786440 | tf_op jit(solution)/shard_map/cond/branch_3_fun/ppermute | solution.py:299
  61.7 3.1 %collective-permute-start.110 = (bf16[32,32,128]{2,1,0:T(8,128)(2,1)S(1)}, bf16[32,32,128]{2,1,0:T(8,128)(2,1)}, u32[]{:S(2)}, u32[]{:S(2)}) collective-permute-start(bf16[32,32,128]{2,1,0:T(8,128)(2,1)S(1)} %get-tuple-element.355), channel_id=1, source_target_pairs={{0,0},{1,1},{2,2},{3,3},{4,4},{5,5},{6,6},{7,7},{8,24},{9,25},{10,... | collective-permute-start | bytes 786440 | tf_op jit(solution)/shard_map/cond/branch_3_fun/ppermute | solution.py:299
  64.9 0.1 collective-permute-start.111
  64.9 0.3 collective-permute-done.108
  65.3 6.6 %collective-permute-done.109 = bf16[16,64,128]{2,1,0:T(8,128)(2,1)} collective-permute-done((bf16[16,64,128]{2,1,0:T(8,128)(2,1)S(1)}, bf16[16,64,128]{2,1,0:T(8,128)(2,1)}, u32[]{:S(2)}, u32[]{:S(2)}) %collective-permute-start.109) | collective-permute-done | bytes 262176 | tf_op jit(solution)/shard_map/cond/branch_3_fun/ppermute | solution.py:299
  71.8 5.5 %collective-permute-done.110 = bf16[32,32,128]{2,1,0:T(8,128)(2,1)} collective-permute-done((bf16[32,32,128]{2,1,0:T(8,128)(2,1)S(1)}, bf16[32,32,128]{2,1,0:T(8,128)(2,1)}, u32[]{:S(2)}, u32[]{:S(2)}) %collective-permute-start.110) | collective-permute-done | bytes 262176 | tf_op jit(solution)/shard_map/cond/branch_3_fun/ppermute | solution.py:299
  77.4 0.0 collective-permute-done.111
  77.4 1.1 %broadcast_select_fusion.5 = (bf16[16,64,128]{2,1,0:T(8,128)(2,1)S(1)}, bf16[16,64,128]{2,1,0:T(8,128)(2,1)S(1)}) fusion(bf16[16,64,128]{2,1,0:T(8,128)(2,1)} %get-tuple-element.453, bf16[16,64,128]{2,1,0:T(8,128)(2,1)} %get-tuple-element.454, pred[]{:T(512)S(6)} %eq.20), kind=kLoop, calls=%fused_computation.16 | loop fusion | flops 262144 | bytes 1048577 | tf_op jit(solution)/shard_map/jit(_where)/select_n | solution.py:378
  78.5 1.1 %broadcast_select_fusion.3 = (bf16[32,32,128]{2,1,0:T(8,128)(2,1)S(1)}, bf16[32,32,128]{2,1,0:T(8,128)(2,1)S(1)}) fusion(bf16[32,32,128]{2,1,0:T(8,128)(2,1)} %get-tuple-element.455, bf16[32,32,128]{2,1,0:T(8,128)(2,1)} %get-tuple-element.456, pred[]{:T(512)S(6)} %eq.20), kind=kLoop, calls=%fused_computation.14 | loop fusion | flops 262144 | bytes 1048577 | tf_op jit(solution)/shard_map/jit(_where)/select_n | solution.py:380
  79.6 0.1 pad_maximum_fusion.3
  79.6 0.1 bitcast_select_fusion.1
  79.8 1.7 %collective-permute-start.195 = (bf16[2048,128]{1,0:T(8,128)(2,1)S(1)}, bf16[2048,128]{1,0:T(8,128)(2,1)S(1)}, u32[]{:S(2)}, u32[]{:S(2)}) collective-permute-start(bf16[2048,128]{1,0:T(8,128)(2,1)S(1)} %bitcast_select_fusion.1), channel_id=1, source_target_pairs={{0,4},{1,5},{2,6},{3,7},{4,0},{5,1},{6,2},{7,3},{8,12},{9,13},{10,... | collective-permute-start | bytes 1572872 | tf_op jit(solution)/shard_map/ppermute | solution.py:299
  81.4 1.5 %collective-permute-done.195 = bf16[2048,128]{1,0:T(8,128)(2,1)S(1)} collective-permute-done((bf16[2048,128]{1,0:T(8,128)(2,1)S(1)}, bf16[2048,128]{1,0:T(8,128)(2,1)S(1)}, u32[]{:S(2)}, u32[]{:S(2)}) %collective-permute-start.195) | collective-permute-done | bytes 524320 | tf_op jit(solution)/shard_map/ppermute | solution.py:299
  83.0 0.2 broadcast_select_fusion.1
  83.1 0.1 pad_maximum_fusion
  83.2 0.1 pad_maximum_fusion.1
  83.3 1.1 %bitcast_select_fusion = bf16[32,128,128]{2,1,0:T(8,128)(2,1)} fusion(bf16[32,128,128]{2,1,0:T(8,128)(2,1)S(1)} %bitcast.34, bf16[32,4,2,16,128]{4,3,2,1,0:T(8,128)(2,1)S(1)} %pad_maximum_fusion.1, pred[]{:T(512)} %bitcast), kind=kLoop, calls=%fused_computation.2 | loop fusion | flops 524288 | bytes 3145729 | tf_op jit(solution)/shard_map/jit(_where)/select_n | solution.py:390
  (3 shorter events, 0.1 us)
Async XLA Ops:
  0.0 1.9 %copy-start = (bf16[32,8,2048]{2,1,0:T(8,128)(2,1)S(1)}, bf16[32,8,2048]{2,1,0:T(8,128)(2,1)}, u32[]{:S(2)}) copy-start(bf16[32,8,2048]{2,1,0:T(8,128)(2,1)} %raw_ref.1) | copy-start | bytes 3145732
  1.2 6.2 %collective-permute-start.192 = (bf16[16,8,2048]{2,1,0:T(8,128)(2,1)S(1)}, bf16[16,8,2048]{2,1,0:T(8,128)(2,1)S(1)}, u32[]{:S(2)}, u32[]{:S(2)}) collective-permute-start(bf16[16,8,2048]{2,1,0:T(8,128)(2,1)S(1)} %constant_dynamic-slice_fusion), channel_id=1, source_target_pairs={{0,4},{1,5},{2,6},{3,7},{4,0},{5,1},{6,2},{7,3},{8,12},{9,13},{10,... | collective-permute-start | bytes 1572872 | tf_op jit(solution)/shard_map/ppermute | solution.py:299
  1.9 44.6 %copy-start.1 = (bf16[256,1024]{1,0:T(8,128)(2,1)S(1)}, bf16[256,1024]{1,0:T(8,128)(2,1)}, u32[]{:S(2)}) copy-start(bf16[256,1024]{1,0:T(8,128)(2,1)} %constant.46.clone.table_ref) | copy-start | bytes 1572868
  8.9 14.5 %collective-permute-start.12 = (bf16[64,16,256]{2,1,0:T(8,128)(2,1)S(1)}, bf16[64,16,256]{2,1,0:T(8,128)(2,1)}, u32[]{:S(2)}, u32[]{:S(2)}) collective-permute-start(bf16[64,16,256]{2,1,0:T(8,128)(2,1)S(1)} %get-tuple-element.299), channel_id=1, source_target_pairs={{0,2},{1,0},{2,3},{3,1},{4,6},{5,4},{6,7},{7,5},{8,10},{9,8},{10,1... | collective-permute-start | bytes 1572872 | tf_op jit(solution)/shard_map/cond/branch_3_fun/ppermute | solution.py:299
  10.2 24.8 %collective-permute-start.13 = (bf16[64,16,256]{2,1,0:T(8,128)(2,1)S(1)}, bf16[64,16,256]{2,1,0:T(8,128)(2,1)}, u32[]{:S(2)}, u32[]{:S(2)}) collective-permute-start(bf16[64,16,256]{2,1,0:T(8,128)(2,1)S(1)} %get-tuple-element.299), channel_id=1, source_target_pairs={{0,0},{1,2},{2,1},{3,3},{4,4},{5,6},{6,5},{7,7},{8,8},{9,10},{10,9... | collective-permute-start | bytes 1572872 | tf_op jit(solution)/shard_map/cond/branch_3_fun/ppermute | solution.py:299
  12.1 26.3 %collective-permute-start.14 = (bf16[64,16,256]{2,1,0:T(8,128)(2,1)S(1)}, bf16[64,16,256]{2,1,0:T(8,128)(2,1)}, u32[]{:S(2)}, u32[]{:S(2)}) collective-permute-start(bf16[64,16,256]{2,1,0:T(8,128)(2,1)S(1)} %get-tuple-element.300), channel_id=1, source_target_pairs={{0,0},{1,1},{2,2},{3,3},{4,4},{5,5},{6,6},{7,7},{8,16},{9,17},{10,... | collective-permute-start | bytes 1572872 | tf_op jit(solution)/shard_map/cond/branch_3_fun/ppermute | solution.py:299
  15.2 23.2 %collective-permute-start.15 = (bf16[64,16,256]{2,1,0:T(8,128)(2,1)S(1)}, bf16[64,16,256]{2,1,0:T(8,128)(2,1)}, u32[]{:S(2)}, u32[]{:S(2)}) collective-permute-start(bf16[64,16,256]{2,1,0:T(8,128)(2,1)S(1)} %get-tuple-element.300), channel_id=1, source_target_pairs={{0,1},{1,0},{2,3},{3,2},{4,5},{5,4},{6,7},{7,6},{8,17},{9,16},{10,... | collective-permute-start | bytes 1572872 | tf_op jit(solution)/shard_map/cond/branch_3_fun/ppermute | solution.py:299
  38.4 6.2 %collective-permute-start.193 = (bf16[64,16,256]{2,1,0:T(8,128)(2,1)}, bf16[64,16,256]{2,1,0:T(8,128)(2,1)S(1)}, u32[]{:S(2)}, u32[]{:S(2)}) collective-permute-start(bf16[64,16,256]{2,1,0:T(8,128)(2,1)} %get-tuple-element.449.b1), channel_id=1, source_target_pairs={{0,4},{1,5},{2,6},{3,7},{4,0},{5,1},{6,2},{7,3},{8,12},{9,13},{10,... | collective-permute-start | bytes 1572872 | tf_op jit(solution)/shard_map/ppermute | solution.py:299
  39.7 6.8 %collective-permute-start.194 = (bf16[64,16,256]{2,1,0:T(8,128)(2,1)}, bf16[64,16,256]{2,1,0:T(8,128)(2,1)S(1)}, u32[]{:S(2)}, u32[]{:S(2)}) collective-permute-start(bf16[64,16,256]{2,1,0:T(8,128)(2,1)} %get-tuple-element.450.b3), channel_id=1, source_target_pairs={{0,4},{1,5},{2,6},{3,7},{4,0},{5,1},{6,2},{7,3},{8,12},{9,13},{10,... | collective-permute-start | bytes 1572872 | tf_op jit(solution)/shard_map/ppermute | solution.py:299
  57.3 7.9 %collective-permute-start.108 = (bf16[16,64,128]{2,1,0:T(8,128)(2,1)S(1)}, bf16[16,64,128]{2,1,0:T(8,128)(2,1)}, u32[]{:S(2)}, u32[]{:S(2)}) collective-permute-start(bf16[16,64,128]{2,1,0:T(8,128)(2,1)S(1)} %get-tuple-element.353), channel_id=1, source_target_pairs={{0,1},{1,3},{2,0},{3,2},{4,5},{5,7},{6,4},{7,6},{8,9},{9,11},{10,8... | collective-permute-start | bytes 786440 | tf_op jit(solution)/shard_map/cond/branch_3_fun/ppermute | solution.py:299
  57.7 14.2 %collective-permute-start.109 = (bf16[16,64,128]{2,1,0:T(8,128)(2,1)S(1)}, bf16[16,64,128]{2,1,0:T(8,128)(2,1)}, u32[]{:S(2)}, u32[]{:S(2)}) collective-permute-start(bf16[16,64,128]{2,1,0:T(8,128)(2,1)S(1)} %get-tuple-element.354), channel_id=1, source_target_pairs={{0,0},{1,2},{2,1},{3,3},{4,4},{5,6},{6,5},{7,7},{8,8},{9,10},{10,9... | collective-permute-start | bytes 786440 | tf_op jit(solution)/shard_map/cond/branch_3_fun/ppermute | solution.py:299
  61.7 15.6 %collective-permute-start.110 = (bf16[32,32,128]{2,1,0:T(8,128)(2,1)S(1)}, bf16[32,32,128]{2,1,0:T(8,128)(2,1)}, u32[]{:S(2)}, u32[]{:S(2)}) collective-permute-start(bf16[32,32,128]{2,1,0:T(8,128)(2,1)S(1)} %get-tuple-element.355), channel_id=1, source_target_pairs={{0,0},{1,1},{2,2},{3,3},{4,4},{5,5},{6,6},{7,7},{8,24},{9,25},{10,... | collective-permute-start | bytes 786440 | tf_op jit(solution)/shard_map/cond/branch_3_fun/ppermute | solution.py:299
  64.9 12.5 %collective-permute-start.111 = (bf16[32,32,128]{2,1,0:T(8,128)(2,1)S(1)}, bf16[32,32,128]{2,1,0:T(8,128)(2,1)}, u32[]{:S(2)}, u32[]{:S(2)}) collective-permute-start(bf16[32,32,128]{2,1,0:T(8,128)(2,1)S(1)} %get-tuple-element.356), channel_id=1, source_target_pairs={{0,1},{1,0},{2,3},{3,2},{4,5},{5,4},{6,7},{7,6},{8,25},{9,24},{10,... | collective-permute-start | bytes 786440 | tf_op jit(solution)/shard_map/cond/branch_3_fun/ppermute | solution.py:299
  79.8 3.2 %collective-permute-start.195 = (bf16[2048,128]{1,0:T(8,128)(2,1)S(1)}, bf16[2048,128]{1,0:T(8,128)(2,1)S(1)}, u32[]{:S(2)}, u32[]{:S(2)}) collective-permute-start(bf16[2048,128]{1,0:T(8,128)(2,1)S(1)} %bitcast_select_fusion.1), channel_id=1, source_target_pairs={{0,4},{1,5},{2,6},{3,7},{4,0},{5,1},{6,2},{7,3},{8,12},{9,13},{10,... | collective-permute-start | bytes 1572872 | tf_op jit(solution)/shard_map/ppermute | solution.py:299

commit v3 on v2

--- a/solution.py
+++ b/solution.py
@@ -197,12 +197,12 @@
     )(order, *[a for a, _ in a_list], *[b for b, _ in b_list], table)
 
 
-def whiten_half(raw, which):
+def whiten_half(raw, info):
     channels, windows, width = raw.shape
     blocks = width // 2 // FINE
     depth = 2 * windows * FINE
 
-    def kernel(which_ref, raw_ref, out_ref, wide_ref):
+    def kernel(info_ref, raw_ref, out_ref, wide_ref):
         whiten_block(raw_ref, out_ref, wide_ref)
 
     return pl.pallas_call(
@@ -210,85 +210,133 @@
         grid_spec=pltpu.PrefetchScalarGridSpec(
             num_scalar_prefetch=1,
             grid=(1,),
-            in_specs=[pl.BlockSpec((ROWS, windows, width), lambda i, which_ref: (which_ref[0], 0, 0))],
+            in_specs=[pl.BlockSpec((ROWS, windows, width), lambda i, info_ref: (info_ref[2], 0, 0))],
             out_specs=pl.BlockSpec((blocks, ROWS, depth), lambda i, *_: (0, 0, 0)),
             scratch_shapes=[pltpu.VMEM((blocks // windows * 2, ROWS * windows, windows * FINE), jnp.float32)],
         ),
         out_shape=jax.ShapeDtypeStruct((blocks, ROWS, depth), jnp.bfloat16),
         compiler_params=pltpu.CompilerParams(vmem_limit_bytes=VMEM_BYTES),
         name="whiten_half",
-    )(which, raw)
-
-
-def whiten_sorted(raw, own, stays):
-    rows, windows, width = raw.shape
+    )(info, raw)
+
+
+def whiten_sorted(raw, own, info):
+    channels, windows, width = raw.shape
     blocks, _, depth = own.shape
 
-    def kernel(stays_ref, raw_ref, own_ref, stay_ref, move_ref, new_ref, wide_ref):
+    def kernel(info_ref, raw_ref, own_ref, stay_ref, move_ref, new_ref, wide_ref):
         whiten_block(raw_ref, new_ref, wide_ref)
 
-        @pl.when(stays_ref[0] == 1)
+        @pl.when(info_ref[3] == 1)
         def _():
             stay_ref[...] = own_ref[...]
             move_ref[...] = new_ref[...]
 
-        @pl.when(stays_ref[0] != 1)
+        @pl.when(info_ref[3] != 1)
         def _():
             stay_ref[...] = new_ref[...]
             move_ref[...] = own_ref[...]
 
     shape = jax.ShapeDtypeStruct(own.shape, jnp.bfloat16)
+    whole = pl.BlockSpec((blocks, ROWS, depth), lambda i, *_: (0, 0, 0))
     return pl.pallas_call(
         kernel,
-        in_specs=[
-            pl.BlockSpec(memory_space=pltpu.SMEM),
-            pl.BlockSpec(memory_space=pltpu.VMEM),
-            pl.BlockSpec(memory_space=pltpu.VMEM),
-        ],
-        out_specs=[pl.BlockSpec(memory_space=pltpu.VMEM)] * 2,
+        grid_spec=pltpu.PrefetchScalarGridSpec(
+            num_scalar_prefetch=1,
+            grid=(1,),
+            in_specs=[pl.BlockSpec((ROWS, windows, width), lambda i, info_ref: (info_ref[2], 0, 0)), whole],
+            out_specs=[whole, whole],
+            scratch_shapes=[
+                pltpu.VMEM(own.shape, jnp.bfloat16),
+                pltpu.VMEM((blocks // windows * 2, ROWS * windows, windows * FINE), jnp.float32),
+            ],
+        ),
         out_shape=[shape, shape],
-        scratch_shapes=[
-            pltpu.VMEM(own.shape, jnp.bfloat16),
-            pltpu.VMEM((blocks // windows * 2, ROWS * windows, windows * FINE), jnp.float32),
-        ],
         compiler_params=pltpu.CompilerParams(vmem_limit_bytes=VMEM_BYTES),
         name="whiten_sorted",
-    )(stays, raw, own)
-
-
-def assign_roles(partner):
+    )(info, raw, own)
+
+
+def assign_roles(partner, members):
     count = partner.shape[0]
     chips = count // 2
 
-    def kernel(partner_ref, out_ref):
+    def kernel(partner_ref, rank_ref, info_ref, moves_ref):
         for group in range(count):
-            out_ref[group] = -1
+            moves_ref[group] = -1
         for group in range(count):
 
-            @pl.when(out_ref[group] < 0)
+            @pl.when(moves_ref[group] < 0)
             def _():
                 def walk(_, here):
                     there = partner_ref[here]
-                    out_ref[here] = 0
-                    out_ref[there] = 1
+                    moves_ref[here] = 0
+                    moves_ref[there] = 1
                     return there ^ 1
 
                 lax.fori_loop(0, chips, walk, jnp.int32(group))
 
-        target = [partner_ref[2 * chip + 1 - out_ref[2 * chip]] // 2 for chip in range(chips)]
+        target = [partner_ref[2 * chip + 1 - moves_ref[2 * chip]] // 2 for chip in range(chips)]
         rank = jnp.int32(0)
         for i in range(chips):
             for j in range(i + 1, chips):
                 rank += jnp.where(target[j] < target[i], math.factorial(chips - 1 - i), 0)
-        out_ref[count] = rank
+        rank_ref[0] = rank
+        group, member = lax.axis_index("group"), lax.axis_index("member")
+        info_ref[0] = jnp.where(member < members // 2, 1, 0)
+        info_ref[1] = member % 2
+        info_ref[2] = group % 2
+        info_ref[3] = 1 - moves_ref[group]
 
     return pl.pallas_call(
         kernel,
         in_specs=[pl.BlockSpec(memory_space=pltpu.SMEM)],
-        out_specs=pl.BlockSpec(memory_space=pltpu.SMEM),
-        out_shape=jax.ShapeDtypeStruct((count + 1,), jnp.int32),
+        out_specs=[pl.BlockSpec(memory_space=pltpu.SMEM)] * 2,
+        out_shape=[jax.ShapeDtypeStruct((1,), jnp.int32), jax.ShapeDtypeStruct((4,), jnp.int32)],
+        scratch_shapes=[pltpu.SMEM((count,), jnp.int32)],
         name="assign_roles",
     )(partner)
+
+
+def assemble(info, pieces, got, members):
+    far, near, here, there = pieces
+    others = 2 * members * ROWS
+    half = others // 2
+
+    def kernel(info_ref, far_ref, near_ref, here_ref, there_ref, got_ref, out_ref):
+        odd, core = info_ref[1], info_ref[2]
+
+        def put_stay(side, low, value):
+            at = pl.multiple_of(side * half, half)
+            out_ref[pl.ds(low, ROWS), pl.ds(at, half), :] = value
+
+        def put_move(side, which, value):
+            for shard in range(2):
+                at = pl.multiple_of(side * half + shard * 2 * ROWS + which * ROWS, ROWS)
+                out_ref[:, pl.ds(at, ROWS), :] = value[:, shard * ROWS : (shard + 1) * ROWS, :]
+
+        @pl.when(info_ref[3] == 1)
+        def _():
+            put_stay(1 - odd, core * ROWS, far_ref[...])
+            put_stay(odd, core * ROWS, near_ref[...])
+            put_stay(1 - odd, (1 - core) * ROWS, got_ref[0].reshape(far.shape))
+            put_stay(odd, (1 - core) * ROWS, got_ref[1].reshape(near.shape))
+
+        @pl.when(info_ref[3] != 1)
+        def _():
+            put_move(odd, core, here_ref[...])
+            put_move(1 - odd, core, there_ref[...])
+            put_move(odd, 1 - core, got_ref[0].reshape(here.shape))
+            put_move(1 - odd, 1 - core, got_ref[1].reshape(there.shape))
+
+    return pl.pallas_call(
+        kernel,
+        in_specs=[pl.BlockSpec(memory_space=pltpu.SMEM)] + [pl.BlockSpec(memory_space=pltpu.VMEM)] * 5,
+        out_specs=pl.BlockSpec(memory_space=pltpu.VMEM),
+        out_shape=jax.ShapeDtypeStruct((2 * ROWS, others, LAGS), jnp.bfloat16),
+        compiler_params=pltpu.CompilerParams(vmem_limit_bytes=VMEM_BYTES),
+        name="assemble",
+    )(info, far, near, here, there, got)
 
 
 def permute(value, groups, members, target):
@@ -321,19 +369,14 @@
 def on_device_pairs(spectra, partner):
     groups, members = lax.axis_size("group"), lax.axis_size("member")
     chips = groups // 2
-    channels, windows, width = spectra.shape
-    group, member = lax.axis_index("group"), lax.axis_index("member")
-    core = group % 2
+    windows, width = spectra.shape[1:]
 
     def across(value):
         return permute(value, groups, members, lambda g, m: (g ^ 1, m))
 
-    roles = assign_roles(partner)
-    rank = roles[groups]
-    stays = 1 - lax.dynamic_slice_in_dim(roles, group, 1)
-    received = across(lax.dynamic_slice_in_dim(spectra, (1 - core) * ROWS, ROWS, 0))
-    own = whiten_half(spectra, core.reshape(1))
-    stay, move = whiten_sorted(received, own, stays)
+    rank, info = assign_roles(partner, members)
+    own = whiten_half(spectra, info)
+    stay, move = whiten_sorted(across(spectra), own, info)
 
     far = (2, 0, 3, 1)
     back = tuple(far.index(m) for m in range(members))
@@ -346,7 +389,7 @@
             second = permute(stay, groups, members, lambda g, m: (g, near[m]))
             same = permute(move, groups, members, lambda g, m: (2 * order[g // 2] + g % 2, m))
             other = permute(move, groups, members, lambda g, m: (2 * order[g // 2] + g % 2, m ^ 1))
-            return first, second, same, other
+            return first, second, same, across(same), other, across(other)
 
         return branch
 
@@ -360,34 +403,23 @@
 
         return branch
 
-    first, second, here, there = lax.switch(rank, [go(order) for order in orders], stay, move)
+    first, second, here, here_too, there, there_too = lax.switch(
+        rank[0], [go(order) for order in orders], stay, move
+    )
     table = jnp.asarray(lag_rows(width // 2, windows))
-    order = jnp.stack([(member < 2).astype(jnp.int32), member % 2, core])
     straight, mirrored = correlate(
-        order,
+        info,
         [(first, 0), (second, 0)],
-        [(here, 0), (across(here), 0), (there, 0), (across(there), 0)],
+        [(here, 0), (here_too, 0), (there, 0), (there_too, 0)],
         table,
         1,
     )
-    from_far, from_near, here, there = lax.switch(
-        rank, [home(order) for order in orders], straight[0], straight[1], mirrored[0], mirrored[1]
+    pieces = lax.switch(
+        rank[0], [home(order) for order in orders], straight[0], straight[1], mirrored[0], mirrored[1]
     )
-
-    even = member % 2 == 0
-    left, right = jnp.where(even, from_near, from_far), jnp.where(even, from_far, from_near)
-    stay_part = jnp.concatenate([left, right], axis=1).reshape(-1, LAGS)
-    left, right = jnp.where(even, here, there), jnp.where(even, there, here)
-    move_part = jnp.concatenate([left, right], axis=1).reshape(-1, LAGS)
-    stay_here = stays[0] == 1
-    keep = jnp.where(stay_here, stay_part, move_part)
-    got = across(jnp.where(stay_here, move_part, stay_part))
-    low, high = jnp.where(core == 0, keep, got), jnp.where(core == 0, got, keep)
-    others = channels * members
-    as_stay = jnp.concatenate([low, high], axis=0).reshape(channels, others, LAGS)
-    shape = (channels, members, 1, ROWS, LAGS)
-    as_move = jnp.concatenate([low.reshape(shape), high.reshape(shape)], axis=2).reshape(channels, others, LAGS)
-    return jnp.where(stay_here, as_stay, as_move)
+    flat = [piece.reshape(-1, LAGS) for piece in pieces]
+    sent = jnp.where(info[3] == 1, jnp.stack(flat[2:]), jnp.stack(flat[:2]))
+    return assemble(info, pieces, across(sent), members)
 
 
 def solution(mesh):

time: 86.1 us -> 82.2 us (0.955)
  the two profiles are of different devices: /device:TPU:19 before, /device:TPU:0 now
where the time goes in v3:
time: 82.2 us; the launch traced here: 83.8 us
  waiting for transfers between devices  30.2 us (37%)
  starting transfers between devices  28.2 us (34%)
  Pallas kernels  18.1 us (22%)
  local copies, waits for them, and re-layouts  4.26 us (5%)
  between operations  1.39 us (2%)
  other arithmetic  1.12 us (1%)
    ppermute x12, waiting for transfers between devices, permute(): return lax.ppermute(value, ('group', 'member'), pairs)  30.2 us
    ppermute x12, starting transfers between devices, permute(): return lax.ppermute(value, ('group', 'member'), pairs)  28.2 us
    pallas_call x1, Pallas kernels, correlate(): pl.pallas_call(correlate_kernel, grid_spec=pltpu.PrefetchScalarGridSpec(n...  10.9 us
    pallas_call x1, Pallas kernels, assemble(): pl.pallas_call(kernel, in_specs=[pl.BlockSpec(memory_space=pltpu.SMEM)] +...  2.09 us
    pallas_call x1, Pallas kernels, whiten_sorted(): pl.pallas_call(kernel, grid_spec=pltpu.PrefetchScalarGridSpec(num_scalar_...  1.97 us
    unnamed x6, local copies, waits for them, and re-layouts  1.89 us
    pallas_call x1, Pallas kernels, whiten_half(): pl.pallas_call(kernel, grid_spec=pltpu.PrefetchScalarGridSpec(num_scalar_...  1.89 us
    cond x4, local copies, waits for them, and re-layouts  1.65 us
  transfers between devices with their start and end apart: 12, of which 5 were waited for; matrix products, arithmetic and copies ran while one was open for 2% of the time, Pallas kernels for 4%

profile of v3, /device:TPU:0, one launch (start us, length us, event | category | flops | bytes accessed | tf_op | source)
XLA Modules:
  0.0 83.8 jit_solution(812966601116990106)
XLA Ops:
  0.0 0.5 collective-permute-start.240
  0.5 1.3 %assign_roles.1 = (s32[1]{0:T(128)}, s32[4]{0:T(128)}) custom-call(s32[8]{0:T(128)} %partner_ref.1), custom_call_target="tpu_custom_call" | custom-call | tf_op jit(solution)/shard_map/assign_roles/pallas_call | solution.py:291
  1.8 0.0 copy-start.2
  1.8 0.7 copy-done.2
  2.4 0.0 copy-start
  2.4 1.2 %copy-done = bf16[32,8,2048]{2,1,0:T(8,128)(2,1)S(1)} copy-done((bf16[32,8,2048]{2,1,0:T(8,128)(2,1)S(1)}, bf16[32,8,2048]{2,1,0:T(8,128)(2,1)}, u32[]{:S(2)}) %copy-start) | copy-done | bytes 1048600
  3.7 1.9 %whiten_half.1.own_ref = bf16[64,16,256]{2,1,0:T(8,128)(2,1)S(1)} custom-call(s32[4]{0:T(128)S(1)} %copy-done.2, bf16[32,8,2048]{2,1,0:T(8,128)(2,1)S(1)} %copy-done), custom_call_target="tpu_custom_call" | custom-call | tf_op jit(solution)/shard_map/whiten_half/pallas_call | solution.py:208
  5.6 0.6 slice.19
  7.5 0.0 copy-start.1
  7.5 0.0 collective-permute-done.240.raw_ref
  7.5 2.0 %whiten_sorted.1 = (bf16[64,16,256]{2,1,0:T(8,128)(2,1)S(1)}, bf16[64,16,256]{2,1,0:T(8,128)(2,1)S(1)}) custom-call(s32[4]{0:T(128)S(1)} %copy-done.2, bf16[32,8,2048]{2,1,0:T(8,128)(2,1)S(1)} %collective-permute-done.240.raw_ref, bf16[64,16,256]{2,1,0:T(8,128)(2,1)S(1)} %whiten_half.1.own_ref), custom_call_target="tpu_custom_call" | custom-call | tf_op jit(solution)/shard_map/whiten_sorted/pallas_call | solution.py:242
  9.5 38.5 %conditional.2 = (bf16[64,16,256]{2,1,0:T(8,128)(2,1)}, bf16[64,16,256]{2,1,0:T(8,128)(2,1)}, bf16[64,16,256]{2,1,0:T(8,128)(2,1)}, bf16[64,16,256]{2,1,0:T(8,12...) conditional(s32[]{:T(128)} %bitcast, ...), branch_computations={%region_0.0_spmd, %region_1.0_spmd, %region_2.0_spmd, %region_3.0_... | conditional | bytes 12583200 | solution.py:406
  9.7 6.8 %collective-permute-start.110 = (bf16[64,16,256]{2,1,0:T(8,128)(2,1)S(1)}, bf16[64,16,256]{2,1,0:T(8,128)(2,1)}, u32[]{:S(2)}, u32[]{:S(2)}) collective-permute-start(bf16[64,16,256]{2,1,0:T(8,128)(2,1)S(1)} %get-tuple-element.350), channel_id=1, source_target_pairs={{0,24},{1,25},{2,26},{3,27},{4,28},{5,29},{6,30},{7,31},{8,0},{9,1... | collective-permute-start | bytes 1572872 | tf_op jit(solution)/shard_map/cond/branch_18_fun/ppermute | solution.py:347
  16.5 5.7 %collective-permute-start.112 = (bf16[64,16,256]{2,1,0:T(8,128)(2,1)S(1)}, bf16[64,16,256]{2,1,0:T(8,128)(2,1)}, u32[]{:S(2)}, u32[]{:S(2)}) collective-permute-start(bf16[64,16,256]{2,1,0:T(8,128)(2,1)S(1)} %get-tuple-element.350), channel_id=1, source_target_pairs={{0,25},{1,24},{2,27},{3,26},{4,29},{5,28},{6,31},{7,30},{8,1},{9,0... | collective-permute-start | bytes 1572872 | tf_op jit(solution)/shard_map/cond/branch_18_fun/ppermute | solution.py:347
  22.2 2.8 %collective-permute-start.108 = (bf16[64,16,256]{2,1,0:T(8,128)(2,1)S(1)}, bf16[64,16,256]{2,1,0:T(8,128)(2,1)}, u32[]{:S(2)}, u32[]{:S(2)}) collective-permute-start(bf16[64,16,256]{2,1,0:T(8,128)(2,1)S(1)} %get-tuple-element.349), channel_id=1, source_target_pairs={{0,2},{1,0},{2,3},{3,1},{4,6},{5,4},{6,7},{7,5},{8,10},{9,8},{10,1... | collective-permute-start | bytes 1572872 | tf_op jit(solution)/shard_map/cond/branch_18_fun/ppermute | solution.py:347
  25.0 1.4 %collective-permute-start.109 = (bf16[64,16,256]{2,1,0:T(8,128)(2,1)S(1)}, bf16[64,16,256]{2,1,0:T(8,128)(2,1)}, u32[]{:S(2)}, u32[]{:S(2)}) collective-permute-start(bf16[64,16,256]{2,1,0:T(8,128)(2,1)S(1)} %get-tuple-element.349), channel_id=1, source_target_pairs={{0,0},{1,2},{2,1},{3,3},{4,4},{5,6},{6,5},{7,7},{8,8},{9,10},{10,9... | collective-permute-start | bytes 1572872 | tf_op jit(solution)/shard_map/cond/branch_18_fun/ppermute | solution.py:347
  26.5 15.5 %collective-permute-done.110 = bf16[64,16,256]{2,1,0:T(8,128)(2,1)} collective-permute-done((bf16[64,16,256]{2,1,0:T(8,128)(2,1)S(1)}, bf16[64,16,256]{2,1,0:T(8,128)(2,1)}, u32[]{:S(2)}, u32[]{:S(2)}) %collective-permute-start.110) | collective-permute-done | bytes 524320 | tf_op jit(solution)/shard_map/cond/branch_18_fun/ppermute | solution.py:347
  42.0 0.0 collective-permute-start.111
  42.0 0.0 collective-permute-done.112
  42.0 0.5 collective-permute-start.113
  42.5 5.3 %collective-permute-done.108 = bf16[64,16,256]{2,1,0:T(8,128)(2,1)} collective-permute-done((bf16[64,16,256]{2,1,0:T(8,128)(2,1)S(1)}, bf16[64,16,256]{2,1,0:T(8,128)(2,1)}, u32[]{:S(2)}, u32[]{:S(2)}) %collective-permute-start.108) | collective-permute-done | bytes 524320 | tf_op jit(solution)/shard_map/cond/branch_18_fun/ppermute | solution.py:347
  47.7 0.0 collective-permute-done.109
  47.7 0.0 collective-permute-done.111
  47.8 0.0 collective-permute-done.113
  48.0 0.0 copy-done.1
  48.0 10.9 %correlate.1 = (bf16[2,16,64,128]{3,2,1,0:T(8,128)(2,1)S(1)}, bf16[2,32,32,128]{3,2,1,0:T(8,128)(2,1)S(1)}) custom-call(s32[4]{0:T(128)S(1)} %copy-done.2, bf16[64,16,256]{2,1,0:T(8,128)(2,1)} %get-tuple-element.473.a1, bf16[64,16,256]{2,1,0:T(8,128)(2,1)} %get-tuple-element.474.a2, bf16[64,16,256]{2,1,0:T(8,128)(2,1)} %get-tuple-element.475.b1, ...), custom_call_target="tpu_custom_call" | custom-call | tf_op jit(solution)/shard_map/correlate/pallas_call | solution.py:170
  59.0 19.6 %conditional.3 = (bf16[16,64,128]{2,1,0:T(8,128)(2,1)}, bf16[16,64,128]{2,1,0:T(8,128)(2,1)S(1)}, bf16[16,64,128]{2,1,0:T(8,128)(2,1)}, bf16[16,64,128]{2,1,0:T(...) conditional(s32[]{:T(128)} %bitcast, ...), branch_computations={%region_24.0_spmd, %region_25.0_spmd, %region_26.0_spmd, %region_2... | conditional | bytes 6291692 | solution.py:417
  59.0 4.4 %collective-permute-start.216 = (bf16[16,64,128]{2,1,0:T(8,128)(2,1)S(1)}, bf16[16,64,128]{2,1,0:T(8,128)(2,1)S(1)}, u32[]{:S(2)}, u32[]{:S(2)}) collective-permute-start(bf16[16,64,128]{2,1,0:T(8,128)(2,1)S(1)} %get-tuple-element.433), channel_id=1, source_target_pairs={{0,1},{1,3},{2,0},{3,2},{4,5},{5,7},{6,4},{7,6},{8,9},{9,11},{10,8... | collective-permute-start | bytes 786440 | tf_op jit(solution)/shard_map/cond/branch_18_fun/ppermute | solution.py:347
  63.4 1.4 %collective-permute-start.217 = (bf16[16,64,128]{2,1,0:T(8,128)(2,1)S(1)}, bf16[16,64,128]{2,1,0:T(8,128)(2,1)}, u32[]{:S(2)}, u32[]{:S(2)}) collective-permute-start(bf16[16,64,128]{2,1,0:T(8,128)(2,1)S(1)} %get-tuple-element.434), channel_id=1, source_target_pairs={{0,0},{1,2},{2,1},{3,3},{4,4},{5,6},{6,5},{7,7},{8,8},{9,10},{10,9... | collective-permute-start | bytes 786440 | tf_op jit(solution)/shard_map/cond/branch_18_fun/ppermute | solution.py:347
  64.8 1.5 %collective-permute-start.218 = (bf16[32,32,128]{2,1,0:T(8,128)(2,1)S(1)}, bf16[32,32,128]{2,1,0:T(8,128)(2,1)}, u32[]{:S(2)}, u32[]{:S(2)}) collective-permute-start(bf16[32,32,128]{2,1,0:T(8,128)(2,1)S(1)} %get-tuple-element.435), channel_id=1, source_target_pairs={{0,8},{1,9},{2,10},{3,11},{4,12},{5,13},{6,14},{7,15},{8,16},{9,17... | collective-permute-start | bytes 786440 | tf_op jit(solution)/shard_map/cond/branch_18_fun/ppermute | solution.py:347
  66.2 3.3 %collective-permute-start.219 = (bf16[32,32,128]{2,1,0:T(8,128)(2,1)S(1)}, bf16[32,32,128]{2,1,0:T(8,128)(2,1)}, u32[]{:S(2)}, u32[]{:S(2)}) collective-permute-start(bf16[32,32,128]{2,1,0:T(8,128)(2,1)S(1)} %get-tuple-element.436), channel_id=1, source_target_pairs={{0,9},{1,8},{2,11},{3,10},{4,13},{5,12},{6,15},{7,14},{8,17},{9,16... | collective-permute-start | bytes 786440 | tf_op jit(solution)/shard_map/cond/branch_18_fun/ppermute | solution.py:347
  69.5 2.3 %collective-permute-done.216 = bf16[16,64,128]{2,1,0:T(8,128)(2,1)S(1)} collective-permute-done((bf16[16,64,128]{2,1,0:T(8,128)(2,1)S(1)}, bf16[16,64,128]{2,1,0:T(8,128)(2,1)S(1)}, u32[]{:S(2)}, u32[]{:S(2)}) %collective-permute-start.216) | collective-permute-done | bytes 262176 | tf_op jit(solution)/shard_map/cond/branch_18_fun/ppermute | solution.py:347
  71.8 0.0 copy-start.21
  71.8 0.7 copy-done.21
  72.5 0.0 collective-permute-done.217
  72.5 1.0 %copy.259 = bf16[16,64,128]{2,1,0:T(8,128)(2,1)S(1)} copy(bf16[16,64,128]{2,1,0:T(8,128)(2,1)} %collective-permute-done.217) | data formatting | bytes 524288 | tf_op jit(solution)/shard_map/cond
  73.4 5.2 %collective-permute-done.218 = bf16[32,32,128]{2,1,0:T(8,128)(2,1)} collective-permute-done((bf16[32,32,128]{2,1,0:T(8,128)(2,1)S(1)}, bf16[32,32,128]{2,1,0:T(8,128)(2,1)}, u32[]{:S(2)}, u32[]{:S(2)}) %collective-permute-start.218) | collective-permute-done | bytes 262176 | tf_op jit(solution)/shard_map/cond/branch_18_fun/ppermute | solution.py:347
  78.6 0.0 collective-permute-done.219
  78.6 1.1 %maximum_select_fusion = bf16[2,1024,128]{2,1,0:T(8,128)(2,1)S(1)} fusion(bf16[1,1024,128]{2,1,0:T(8,128)(2,1)} %bitcast.7, bf16[1,1024,128]{2,1,0:T(8,128)(2,1)} %bitcast.6, bf16[1,1024,128]{2,1,0:T(8,128)(2,1)S(1)} %bitcast.15, bf16[1,1024,128]{2,1,0:T(8,128)(2,1)S(1)} %bitcast.14, pred[]{:T(512)} %bitcast.5), kind=kLoop, calls=%fused_computation | loop fusion | flops 786432 | bytes 1572865 | tf_op jit(solution)/shard_map/jit(_where)/select_n | solution.py:421
  79.7 0.1 collective-permute-start.241
  79.8 1.9 %collective-permute-done.241.got_ref = bf16[2,1024,128]{2,1,0:T(8,128)(2,1)S(1)} collective-permute-done((bf16[2,1024,128]{2,1,0:T(8,128)(2,1)S(1)}, bf16[2,1024,128]{2,1,0:T(8,128)(2,1)S(1)}, u32[]{:S(2)}, u32[]{:S(2)}) %collective-permute-start.241) | collective-permute-done | bytes 524320 | tf_op jit(solution)/shard_map/ppermute | solution.py:347
  81.7 2.1 %assemble.1 = bf16[32,128,128]{2,1,0:T(8,128)(2,1)} custom-call(s32[4]{0:T(128)S(1)} %copy-done.2, bf16[16,64,128]{2,1,0:T(8,128)(2,1)S(1)} %get-tuple-element.490.far_ref, bf16[16,64,128]{2,1,0:T(8,128)(2,1)S(1)} %get-tuple-element.492.near_ref, bf16[32,32,128]{2,1,0:T(8,128)(2,1)} %get-tuple-element.493.here_ref, ...), custom_call_target="tpu_custom_call" | custom-call | tf_op jit(solution)/shard_map/assemble/pallas_call | solution.py:332
  (3 shorter events, 0.1 us)
Async XLA Ops:
  0.0 7.5 %collective-permute-start.240 = (bf16[32,8,2048]{2,1,0:T(8,128)(2,1)}, bf16[32,8,2048]{2,1,0:T(8,128)(2,1)S(1)}, u32[]{:S(2)}, u32[]{:S(2)}) collective-permute-start(bf16[32,8,2048]{2,1,0:T(8,128)(2,1)} %raw_ref.1), channel_id=1, source_target_pairs={{0,4},{1,5},{2,6},{3,7},{4,0},{5,1},{6,2},{7,3},{8,12},{9,13},{10,... | collective-permute-start | bytes 3145736 | tf_op jit(solution)/shard_map/ppermute | solution.py:347
  1.8 0.7 copy-start.2
  2.4 1.2 %copy-start = (bf16[32,8,2048]{2,1,0:T(8,128)(2,1)S(1)}, bf16[32,8,2048]{2,1,0:T(8,128)(2,1)}, u32[]{:S(2)}) copy-start(bf16[32,8,2048]{2,1,0:T(8,128)(2,1)} %raw_ref.1) | copy-start | bytes 3145732
  7.5 40.5 %copy-start.1 = (bf16[256,1024]{1,0:T(8,128)(2,1)S(1)}, bf16[256,1024]{1,0:T(8,128)(2,1)}, u32[]{:S(2)}) copy-start(bf16[256,1024]{1,0:T(8,128)(2,1)} %constant.11.clone.table_ref) | copy-start | bytes 1572868
  9.7 32.3 %collective-permute-start.110 = (bf16[64,16,256]{2,1,0:T(8,128)(2,1)S(1)}, bf16[64,16,256]{2,1,0:T(8,128)(2,1)}, u32[]{:S(2)}, u32[]{:S(2)}) collective-permute-start(bf16[64,16,256]{2,1,0:T(8,128)(2,1)S(1)} %get-tuple-element.350), channel_id=1, source_target_pairs={{0,24},{1,25},{2,26},{3,27},{4,28},{5,29},{6,30},{7,31},{8,0},{9,1... | collective-permute-start | bytes 1572872 | tf_op jit(solution)/shard_map/cond/branch_18_fun/ppermute | solution.py:347
  16.5 25.5 %collective-permute-start.112 = (bf16[64,16,256]{2,1,0:T(8,128)(2,1)S(1)}, bf16[64,16,256]{2,1,0:T(8,128)(2,1)}, u32[]{:S(2)}, u32[]{:S(2)}) collective-permute-start(bf16[64,16,256]{2,1,0:T(8,128)(2,1)S(1)} %get-tuple-element.350), channel_id=1, source_target_pairs={{0,25},{1,24},{2,27},{3,26},{4,29},{5,28},{6,31},{7,30},{8,1},{9,0... | collective-permute-start | bytes 1572872 | tf_op jit(solution)/shard_map/cond/branch_18_fun/ppermute | solution.py:347
  22.2 25.5 %collective-permute-start.108 = (bf16[64,16,256]{2,1,0:T(8,128)(2,1)S(1)}, bf16[64,16,256]{2,1,0:T(8,128)(2,1)}, u32[]{:S(2)}, u32[]{:S(2)}) collective-permute-start(bf16[64,16,256]{2,1,0:T(8,128)(2,1)S(1)} %get-tuple-element.349), channel_id=1, source_target_pairs={{0,2},{1,0},{2,3},{3,1},{4,6},{5,4},{6,7},{7,5},{8,10},{9,8},{10,1... | collective-permute-start | bytes 1572872 | tf_op jit(solution)/shard_map/cond/branch_18_fun/ppermute | solution.py:347
  25.0 22.7 %collective-permute-start.109 = (bf16[64,16,256]{2,1,0:T(8,128)(2,1)S(1)}, bf16[64,16,256]{2,1,0:T(8,128)(2,1)}, u32[]{:S(2)}, u32[]{:S(2)}) collective-permute-start(bf16[64,16,256]{2,1,0:T(8,128)(2,1)S(1)} %get-tuple-element.349), channel_id=1, source_target_pairs={{0,0},{1,2},{2,1},{3,3},{4,4},{5,6},{6,5},{7,7},{8,8},{9,10},{10,9... | collective-permute-start | bytes 1572872 | tf_op jit(solution)/shard_map/cond/branch_18_fun/ppermute | solution.py:347
  42.0 5.8 %collective-permute-start.111 = (bf16[64,16,256]{2,1,0:T(8,128)(2,1)}, bf16[64,16,256]{2,1,0:T(8,128)(2,1)}, u32[]{:S(2)}, u32[]{:S(2)}) collective-permute-start(bf16[64,16,256]{2,1,0:T(8,128)(2,1)} %collective-permute-done.110), channel_id=1, source_target_pairs={{0,4},{1,5},{2,6},{3,7},{4,0},{5,1},{6,2},{7,3},{8,12},{9,13},{10,... | collective-permute-start | bytes 1572872 | tf_op jit(solution)/shard_map/cond/branch_18_fun/ppermute | solution.py:347
  42.0 5.8 %collective-permute-start.113 = (bf16[64,16,256]{2,1,0:T(8,128)(2,1)}, bf16[64,16,256]{2,1,0:T(8,128)(2,1)}, u32[]{:S(2)}, u32[]{:S(2)}) collective-permute-start(bf16[64,16,256]{2,1,0:T(8,128)(2,1)} %collective-permute-done.112), channel_id=1, source_target_pairs={{0,4},{1,5},{2,6},{3,7},{4,0},{5,1},{6,2},{7,3},{8,12},{9,13},{10,... | collective-permute-start | bytes 1572872 | tf_op jit(solution)/shard_map/cond/branch_18_fun/ppermute | solution.py:347
  59.0 12.8 %collective-permute-start.216 = (bf16[16,64,128]{2,1,0:T(8,128)(2,1)S(1)}, bf16[16,64,128]{2,1,0:T(8,128)(2,1)S(1)}, u32[]{:S(2)}, u32[]{:S(2)}) collective-permute-start(bf16[16,64,128]{2,1,0:T(8,128)(2,1)S(1)} %get-tuple-element.433), channel_id=1, source_target_pairs={{0,1},{1,3},{2,0},{3,2},{4,5},{5,7},{6,4},{7,6},{8,9},{9,11},{10,8... | collective-permute-start | bytes 786440 | tf_op jit(solution)/shard_map/cond/branch_18_fun/ppermute | solution.py:347
  63.4 9.1 %collective-permute-start.217 = (bf16[16,64,128]{2,1,0:T(8,128)(2,1)S(1)}, bf16[16,64,128]{2,1,0:T(8,128)(2,1)}, u32[]{:S(2)}, u32[]{:S(2)}) collective-permute-start(bf16[16,64,128]{2,1,0:T(8,128)(2,1)S(1)} %get-tuple-element.434), channel_id=1, source_target_pairs={{0,0},{1,2},{2,1},{3,3},{4,4},{5,6},{6,5},{7,7},{8,8},{9,10},{10,9... | collective-permute-start | bytes 786440 | tf_op jit(solution)/shard_map/cond/branch_18_fun/ppermute | solution.py:347
  64.8 13.9 %collective-permute-start.218 = (bf16[32,32,128]{2,1,0:T(8,128)(2,1)S(1)}, bf16[32,32,128]{2,1,0:T(8,128)(2,1)}, u32[]{:S(2)}, u32[]{:S(2)}) collective-permute-start(bf16[32,32,128]{2,1,0:T(8,128)(2,1)S(1)} %get-tuple-element.435), channel_id=1, source_target_pairs={{0,8},{1,9},{2,10},{3,11},{4,12},{5,13},{6,14},{7,15},{8,16},{9,17... | collective-permute-start | bytes 786440 | tf_op jit(solution)/shard_map/cond/branch_18_fun/ppermute | solution.py:347
  66.2 12.4 %collective-permute-start.219 = (bf16[32,32,128]{2,1,0:T(8,128)(2,1)S(1)}, bf16[32,32,128]{2,1,0:T(8,128)(2,1)}, u32[]{:S(2)}, u32[]{:S(2)}) collective-permute-start(bf16[32,32,128]{2,1,0:T(8,128)(2,1)S(1)} %get-tuple-element.436), channel_id=1, source_target_pairs={{0,9},{1,8},{2,11},{3,10},{4,13},{5,12},{6,15},{7,14},{8,17},{9,16... | collective-permute-start | bytes 786440 | tf_op jit(solution)/shard_map/cond/branch_18_fun/ppermute | solution.py:347
  71.8 0.7 copy-start.21
  79.7 2.0 %collective-permute-start.241 = (bf16[2,1024,128]{2,1,0:T(8,128)(2,1)S(1)}, bf16[2,1024,128]{2,1,0:T(8,128)(2,1)S(1)}, u32[]{:S(2)}, u32[]{:S(2)}) collective-permute-start(bf16[2,1024,128]{2,1,0:T(8,128)(2,1)S(1)} %maximum_select_fusion), channel_id=1, source_target_pairs={{0,4},{1,5},{2,6},{3,7},{4,0},{5,1},{6,2},{7,3},{8,12},{9,13},{10,... | collective-permute-start | bytes 1572872 | tf_op jit(solution)/shard_map/ppermute | solution.py:347

commit v4 on v3

--- a/solution.py
+++ b/solution.py
@@ -104,9 +104,12 @@
     b_count = 4 * ROWS
     width = 2 * b_count
     swap_a, swap_b, first_half = order_ref[0], order_ref[1], order_ref[2]
-    fine_row = lax.broadcasted_iota(jnp.int32, (FINE, depth), 0)
-    fine_lane = lax.broadcasted_iota(jnp.int32, (FINE, depth), 1) % FINE
-    mask = (fine_row == fine_lane).astype(jnp.float32)
+    part = FINE // 2
+    lane = lax.broadcasted_iota(jnp.int32, (part, depth), 1)
+    mask = (lane % part == lax.broadcasted_iota(jnp.int32, (part, depth), 0)).astype(jnp.float32)
+    upper = (lax.broadcasted_iota(jnp.int32, (ROWS, depth), 1) // part % 2).astype(jnp.float32)
+    upper = upper.astype(jnp.bfloat16)
+    sides = (1 - upper, upper)
 
     for index, ref in enumerate((a1, a2)):
         at = pl.multiple_of((index ^ swap_a) * ROWS, ROWS)
@@ -117,21 +120,23 @@
         at = pl.multiple_of(spot * ROWS, ROWS)
         for f in range(chunk):
             value = ref[f]
-            rhs_ref[f, pl.ds(at, ROWS), :] = value
-            rhs_ref[f, pl.ds(b_count + at, ROWS), :half] = -value[:, half:]
-            rhs_ref[f, pl.ds(b_count + at, ROWS), half:] = value[:, :half]
+            turned = jnp.concatenate([-value[:, half:], value[:, :half]], axis=1)
+            for side in range(2):
+                rhs_ref[f, pl.ds(side * width + at, ROWS), :] = value * sides[side]
+                rhs_ref[f, pl.ds(side * width + b_count + at, ROWS), :] = turned * sides[side]
     for f in range(chunk):
         parts = []
         for i in range(a_count):
-            row = jnp.broadcast_to(rows_ref[f, i : i + 1, :], (FINE, depth))
-            parts.append((row * mask).astype(jnp.bfloat16))
-        left = jnp.concatenate(parts, axis=0)
+            parts.append(jnp.broadcast_to(rows_ref[f, i : i + 1, :], (part, depth)) * mask)
+        left = jnp.concatenate(parts, axis=0).astype(jnp.bfloat16)
         cross = lax.dot_general(
             left, rhs_ref[f], (((1,), (1,)), ((), ())), preferred_element_type=jnp.float32
-        ).astype(jnp.bfloat16)
+        )
         at = pl.multiple_of((step * chunk + f) * FINE, FINE)
         for i in range(a_count):
-            cross_ref[pl.ds(at, FINE), i * width : (i + 1) * width] = cross[i * FINE : (i + 1) * FINE]
+            rows = cross[i * part : (i + 1) * part]
+            both = jnp.concatenate([rows[:, :width], rows[:, width:]], axis=0)
+            cross_ref[pl.ds(at, FINE), i * width : (i + 1) * width] = both.astype(jnp.bfloat16)
 
     @pl.when(step == pl.num_programs(1) - 1)
     def _():
@@ -149,12 +154,13 @@
                     pltpu.roll(cos_part, b_count, axis=1) - sin_part,
                 )
                 turned = joined.T
-                own_ref[(i // ROWS) ^ swap_a, i % ROWS] = turned[:b_count].astype(jnp.bfloat16)
+                at = i % ROWS * b_count
+                own_ref[(i // ROWS) ^ swap_a, at : at + b_count, :] = turned[:b_count].astype(jnp.bfloat16)
                 flip_ref[pl.ds(i, b_count, stride=a_count), :] = turned[b_count:]
         span = b_count // 2 * a_count
         for index in range(2):
             value = flip_ref[index * span : (index + 1) * span, :].astype(jnp.bfloat16)
-            other_ref[index ^ swap_b] = value.reshape(b_count // 2, a_count, LAGS)
+            other_ref[index ^ swap_b] = value
 
 
 def correlate(order, a_list, b_list, table, b_blocks, chunk=16):
@@ -176,19 +182,19 @@
             + [spec(o, stride) for _, o in b_list]
             + [pl.BlockSpec((2 * LAGS, freqs), lambda j, s, *_: (0, 0))],
             out_specs=[
-                pl.BlockSpec((2, ROWS, b_count, LAGS), lambda j, s, *_: (0, 0, j, 0)),
-                pl.BlockSpec((2, b_count // 2, a_count, LAGS), lambda j, s, *_: (0, j, 0, 0)),
+                pl.BlockSpec((2, ROWS * b_count, LAGS), lambda j, s, *_: (0, j, 0)),
+                pl.BlockSpec((2, b_count // 2 * a_count, LAGS), lambda j, s, *_: (0, j, 0)),
             ],
             scratch_shapes=[
                 pltpu.VMEM((chunk, a_count, depth), jnp.float32),
-                pltpu.VMEM((chunk, width, depth), jnp.bfloat16),
+                pltpu.VMEM((chunk, 2 * width, depth), jnp.bfloat16),
                 pltpu.VMEM((freqs, a_count * width), jnp.bfloat16),
                 pltpu.VMEM((b_count * a_count, LAGS), jnp.float32),
             ],
         ),
         out_shape=[
-            jax.ShapeDtypeStruct((2, ROWS, b_blocks * b_count, LAGS), jnp.bfloat16),
-            jax.ShapeDtypeStruct((2, b_blocks * b_count // 2, a_count, LAGS), jnp.bfloat16),
+            jax.ShapeDtypeStruct((2, b_blocks * ROWS * b_count, LAGS), jnp.bfloat16),
+            jax.ShapeDtypeStruct((2, b_blocks * b_count // 2 * a_count, LAGS), jnp.bfloat16),
         ],
         compiler_params=pltpu.CompilerParams(
             vmem_limit_bytes=VMEM_BYTES, dimension_semantics=("arbitrary", "arbitrary")
@@ -202,19 +208,23 @@
     blocks = width // 2 // FINE
     depth = 2 * windows * FINE
 
-    def kernel(info_ref, raw_ref, out_ref, wide_ref):
-        whiten_block(raw_ref, out_ref, wide_ref)
+    def kernel(info_ref, raw_ref, out_ref, half_ref, wide_ref, sem):
+        low = pl.multiple_of(info_ref[2] * ROWS, ROWS)
+        copy = pltpu.make_async_copy(raw_ref.at[pl.ds(low, ROWS)], half_ref, sem)
+        copy.start()
+        copy.wait()
+        whiten_block(half_ref, out_ref, wide_ref)
 
     return pl.pallas_call(
         kernel,
-        grid_spec=pltpu.PrefetchScalarGridSpec(
-            num_scalar_prefetch=1,
-            grid=(1,),
-            in_specs=[pl.BlockSpec((ROWS, windows, width), lambda i, info_ref: (info_ref[2], 0, 0))],
-            out_specs=pl.BlockSpec((blocks, ROWS, depth), lambda i, *_: (0, 0, 0)),
-            scratch_shapes=[pltpu.VMEM((blocks // windows * 2, ROWS * windows, windows * FINE), jnp.float32)],
-        ),
+        in_specs=[pl.BlockSpec(memory_space=pltpu.SMEM), pl.BlockSpec(memory_space=pltpu.HBM)],
+        out_specs=pl.BlockSpec(memory_space=pltpu.VMEM),
         out_shape=jax.ShapeDtypeStruct((blocks, ROWS, depth), jnp.bfloat16),
+        scratch_shapes=[
+            pltpu.VMEM((ROWS, windows, width), jnp.bfloat16),
+            pltpu.VMEM((blocks // windows * 2, ROWS * windows, windows * FINE), jnp.float32),
+            pltpu.SemaphoreType.DMA(()),
+        ],
         compiler_params=pltpu.CompilerParams(vmem_limit_bytes=VMEM_BYTES),
         name="whiten_half",
     )(info, raw)
@@ -299,35 +309,36 @@
 
 
 def assemble(info, pieces, got, members):
-    far, near, here, there = pieces
     others = 2 * members * ROWS
     half = others // 2
 
     def kernel(info_ref, far_ref, near_ref, here_ref, there_ref, got_ref, out_ref):
         odd, core = info_ref[1], info_ref[2]
 
-        def put_stay(side, low, value):
+        def put_stay(side, which, ref):
+            low = pl.multiple_of(which * ROWS, ROWS)
             at = pl.multiple_of(side * half, half)
-            out_ref[pl.ds(low, ROWS), pl.ds(at, half), :] = value
-
-        def put_move(side, which, value):
+            out_ref[pl.ds(low, ROWS), pl.ds(at, half), :] = ref[...].reshape(ROWS, half, LAGS)
+
+        def put_move(side, which, ref):
+            value = ref[...].reshape(2 * ROWS, 2 * ROWS, LAGS)
             for shard in range(2):
                 at = pl.multiple_of(side * half + shard * 2 * ROWS + which * ROWS, ROWS)
                 out_ref[:, pl.ds(at, ROWS), :] = value[:, shard * ROWS : (shard + 1) * ROWS, :]
 
         @pl.when(info_ref[3] == 1)
         def _():
-            put_stay(1 - odd, core * ROWS, far_ref[...])
-            put_stay(odd, core * ROWS, near_ref[...])
-            put_stay(1 - odd, (1 - core) * ROWS, got_ref[0].reshape(far.shape))
-            put_stay(odd, (1 - core) * ROWS, got_ref[1].reshape(near.shape))
+            put_stay(1 - odd, core, far_ref)
+            put_stay(odd, core, near_ref)
+            put_stay(1 - odd, 1 - core, got_ref.at[0])
+            put_stay(odd, 1 - core, got_ref.at[1])
 
         @pl.when(info_ref[3] != 1)
         def _():
-            put_move(odd, core, here_ref[...])
-            put_move(1 - odd, core, there_ref[...])
-            put_move(odd, 1 - core, got_ref[0].reshape(here.shape))
-            put_move(1 - odd, 1 - core, got_ref[1].reshape(there.shape))
+            put_move(odd, core, here_ref)
+            put_move(1 - odd, core, there_ref)
+            put_move(odd, 1 - core, got_ref.at[0])
+            put_move(1 - odd, 1 - core, got_ref.at[1])
 
     return pl.pallas_call(
         kernel,
@@ -336,7 +347,7 @@
         out_shape=jax.ShapeDtypeStruct((2 * ROWS, others, LAGS), jnp.bfloat16),
         compiler_params=pltpu.CompilerParams(vmem_limit_bytes=VMEM_BYTES),
         name="assemble",
-    )(info, far, near, here, there, got)
+    )(info, *pieces, got)
 
 
 def permute(value, groups, members, target):
@@ -363,7 +374,8 @@
     result, _ = correlate(
         order, [(white, 0), (white, 1)], [(theirs, q) for q in range(4)], table, others // (4 * ROWS)
     )
-    return result.reshape(channels, others, LAGS)
+    result = result.reshape(2, others // (4 * ROWS), ROWS, 4 * ROWS, LAGS)
+    return jnp.transpose(result, (0, 2, 1, 3, 4)).reshape(channels, others, LAGS)
 
 
 def on_device_pairs(spectra, partner):
@@ -383,23 +395,41 @@
     near = (0, 2, 1, 3)
     orders = list(itertools.permutations(range(chips)))
 
+    def straight_way(order):
+        return sum(order[chip] == chips - 1 - chip for chip in range(chips)) < 2
+
     def go(order):
         def branch(stay, move):
+            def go_on(value, flip):
+                return permute(value, groups, members, lambda g, m: (2 * order[g // 2] + g % 2, m ^ flip))
+
+            here = go_on(move, 0)
             first = permute(stay, groups, members, lambda g, m: (g, far[m]))
+            if straight_way(order):
+                there = go_on(move, 1)
+            else:
+                barred, _, stay = lax.optimization_barrier((here, first, stay))
+                there = permute(barred, groups, members, lambda g, m: (g, m ^ 1))
             second = permute(stay, groups, members, lambda g, m: (g, near[m]))
-            same = permute(move, groups, members, lambda g, m: (2 * order[g // 2] + g % 2, m))
-            other = permute(move, groups, members, lambda g, m: (2 * order[g // 2] + g % 2, m ^ 1))
-            return first, second, same, across(same), other, across(other)
+            return first, second, here, across(here), there, across(there)
 
         return branch
 
     def home(order):
         def branch(first, second, same, other):
-            first = permute(first, groups, members, lambda g, m: (g, back[m]))
-            second = permute(second, groups, members, lambda g, m: (g, near[m]))
-            same = permute(same, groups, members, lambda g, m: (2 * order.index(g // 2) + g % 2, m))
-            other = permute(other, groups, members, lambda g, m: (2 * order.index(g // 2) + g % 2, m ^ 1))
-            return first, second, same, other
+            def back_home(value, flip):
+                return permute(value, groups, members, lambda g, m: (2 * order.index(g // 2) + g % 2, m ^ flip))
+
+            here = back_home(same, 0)
+            from_near = permute(second, groups, members, lambda g, m: (g, near[m]))
+            if straight_way(order):
+                there = back_home(other, 1)
+            else:
+                swapped = permute(other, groups, members, lambda g, m: (g, m ^ 1))
+                first, swapped, _, _ = lax.optimization_barrier((first, swapped, from_near, here))
+                there = back_home(swapped, 0)
+            from_far = permute(first, groups, members, lambda g, m: (g, back[m]))
+            return from_far, from_near, here, there
 
         return branch
 
@@ -417,8 +447,8 @@
     pieces = lax.switch(
         rank[0], [home(order) for order in orders], straight[0], straight[1], mirrored[0], mirrored[1]
     )
-    flat = [piece.reshape(-1, LAGS) for piece in pieces]
-    sent = jnp.where(info[3] == 1, jnp.stack(flat[2:]), jnp.stack(flat[:2]))
+    far_piece, near_piece, here_piece, there_piece = pieces
+    sent = jnp.where(info[3] == 1, jnp.stack([here_piece, there_piece]), jnp.stack([far_piece, near_piece]))
     return assemble(info, pieces, across(sent), members)
 
 

time: 82.2 us -> 78.5 us (0.955); the launches traced: 83.8 us -> 79.2 us
  starting transfers between devices: 28.2 us -> 16 us
  waiting for transfers between devices: 30.2 us -> 39.9 us
  Pallas kernels: 18.1 us -> 16.4 us
    ppermute x12 -> x13, starting transfers between devices: 28.2 us -> 16 us  [permute(): return lax.ppermute(value, ('group', 'member'), pairs)]
    ppermute x12 -> x13, waiting for transfers between devices: 30.2 us -> 39.9 us  [permute(): return lax.ppermute(value, ('group', 'member'), pairs)]
    pallas_call x1, Pallas kernels: 10.9 us -> 9.11 us  [correlate(): pl.pallas_call(correlate_kernel, grid_spec=pltpu.PrefetchScalarGridSpec(n...]
    cond x4 -> x2, local copies, waits for them, and re-layouts: 1.65 us -> 1.9 us
  transfers between devices with their start and end apart: 12 -> 13, of which waited for: 5 -> 8; matrix products, arithmetic and copies ran while one was open for 2% -> 3% of each run, Pallas kernels for 4% -> 4%
where the time goes in v4:
time: 78.5 us; the launch traced here: 79.2 us
  waiting for transfers between devices  39.9 us (51%)
  Pallas kernels  16.4 us (21%)
  starting transfers between devices  16 us (20%)
  local copies, waits for them, and re-layouts  4.36 us (6%)
  between operations  1.29 us (2%)
  other arithmetic  1.12 us (1%)
    ppermute x13, waiting for transfers between devices, permute(): return lax.ppermute(value, ('group', 'member'), pairs)  39.9 us
    ppermute x13, starting transfers between devices, permute(): return lax.ppermute(value, ('group', 'member'), pairs)  16 us
    pallas_call x1, Pallas kernels, correlate(): pl.pallas_call(correlate_kernel, grid_spec=pltpu.PrefetchScalarGridSpec(n...  9.11 us
    pallas_call x1, Pallas kernels, assemble(): pl.pallas_call(kernel, in_specs=[pl.BlockSpec(memory_space=pltpu.SMEM)] +...  2.09 us
    pallas_call x1, Pallas kernels, whiten_sorted(): pl.pallas_call(kernel, grid_spec=pltpu.PrefetchScalarGridSpec(num_scalar_...  1.97 us
    pallas_call x1, Pallas kernels, whiten_half(): pl.pallas_call(kernel, in_specs=[pl.BlockSpec(memory_space=pltpu.SMEM), p...  1.95 us
    cond x2, local copies, waits for them, and re-layouts  1.9 us
    unnamed x6, local copies, waits for them, and re-layouts  1.82 us
  transfers between devices with their start and end apart: 13, of which 8 were waited for; matrix products, arithmetic and copies ran while one was open for 3% of the time, Pallas kernels for 4%

profile of v4, /device:TPU:0, one launch (start us, length us, event | category | flops | bytes accessed | tf_op | source)
XLA Modules:
  0.0 79.2 jit_solution(16294613118931532263)
XLA Ops:
  0.0 0.5 collective-permute-start.247
  0.5 1.3 %assign_roles.1 = (s32[1]{0:T(128)}, s32[4]{0:T(128)}) custom-call(s32[8]{0:T(128)} %partner_ref.1), custom_call_target="tpu_custom_call" | custom-call | tf_op jit(solution)/shard_map/assign_roles/pallas_call | solution.py:301
  1.8 0.0 copy-start.2
  1.8 0.6 copy-done.2
  2.4 0.0 copy-start
  2.4 1.2 %copy-done = bf16[32,8,2048]{2,1,0:T(8,128)(2,1)S(1)} copy-done((bf16[32,8,2048]{2,1,0:T(8,128)(2,1)S(1)}, bf16[32,8,2048]{2,1,0:T(8,128)(2,1)}, u32[]{:S(2)}) %copy-start) | copy-done | bytes 1048600
  3.6 2.0 %whiten_half.1.own_ref = bf16[64,16,256]{2,1,0:T(8,128)(2,1)S(1)} custom-call(s32[4]{0:T(128)S(1)} %copy-done.2, bf16[32,8,2048]{2,1,0:T(8,128)(2,1)S(1)} %copy-done), custom_call_target="tpu_custom_call" | custom-call | tf_op jit(solution)/shard_map/whiten_half/pallas_call | solution.py:218
  5.6 0.6 slice.19
  7.3 0.0 copy-start.1
  7.4 0.0 collective-permute-done.247.raw_ref
  7.4 2.0 %whiten_sorted.1 = (bf16[64,16,256]{2,1,0:T(8,128)(2,1)S(1)}, bf16[64,16,256]{2,1,0:T(8,128)(2,1)S(1)}) custom-call(s32[4]{0:T(128)S(1)} %copy-done.2, bf16[32,8,2048]{2,1,0:T(8,128)(2,1)S(1)} %collective-permute-done.247.raw_ref, bf16[64,16,256]{2,1,0:T(8,128)(2,1)S(1)} %whiten_half.1.own_ref), custom_call_target="tpu_custom_call" | custom-call | tf_op jit(solution)/shard_map/whiten_sorted/pallas_call | solution.py:252
  9.3 34.5 %conditional.2 = (bf16[64,16,256]{2,1,0:T(8,128)(2,1)}, bf16[64,16,256]{2,1,0:T(8,128)(2,1)}, bf16[64,16,256]{2,1,0:T(8,128)(2,1)}, bf16[64,16,256]{2,1,0:T(8,12...) conditional(s32[]{:T(128)} %bitcast, ...), branch_computations={%region_0.0_spmd, %region_1.0_spmd, %region_2.0_spmd, %region_3.0_... | conditional | bytes 12583200 | solution.py:436
  9.4 3.6 %collective-permute-start.102 = (bf16[64,16,256]{2,1,0:T(8,128)(2,1)S(1)}, bf16[64,16,256]{2,1,0:T(8,128)(2,1)}, u32[]{:S(2)}, u32[]{:S(2)}) collective-permute-start(bf16[64,16,256]{2,1,0:T(8,128)(2,1)S(1)} %get-tuple-element.353), channel_id=1, source_target_pairs={{0,2},{1,0},{2,3},{3,1},{4,6},{5,4},{6,7},{7,5},{8,10},{9,8},{10,1... | collective-permute-start | bytes 1572872 | tf_op jit(solution)/shard_map/cond/branch_17_fun/ppermute | solution.py:358
  13.0 1.5 %collective-permute-start.103 = (bf16[64,16,256]{2,1,0:T(8,128)(2,1)S(1)}, bf16[64,16,256]{2,1,0:T(8,128)(2,1)}, u32[]{:S(2)}, u32[]{:S(2)}) collective-permute-start(bf16[64,16,256]{2,1,0:T(8,128)(2,1)S(1)} %get-tuple-element.352), channel_id=1, source_target_pairs={{0,16},{1,17},{2,18},{3,19},{4,20},{5,21},{6,22},{7,23},{8,24},{9,... | collective-permute-start | bytes 1572872 | tf_op jit(solution)/shard_map/cond/branch_17_fun/ppermute | solution.py:358
  14.5 10.3 %collective-permute-done.102 = bf16[64,16,256]{2,1,0:T(8,128)(2,1)} collective-permute-done((bf16[64,16,256]{2,1,0:T(8,128)(2,1)S(1)}, bf16[64,16,256]{2,1,0:T(8,128)(2,1)}, u32[]{:S(2)}, u32[]{:S(2)}) %collective-permute-start.102) | collective-permute-done | bytes 524320 | tf_op jit(solution)/shard_map/cond/branch_17_fun/ppermute | solution.py:358
  24.9 3.2 %collective-permute-done.103 = bf16[64,16,256]{2,1,0:T(8,128)(2,1)} collective-permute-done((bf16[64,16,256]{2,1,0:T(8,128)(2,1)S(1)}, bf16[64,16,256]{2,1,0:T(8,128)(2,1)}, u32[]{:S(2)}, u32[]{:S(2)}) %collective-permute-start.103) | collective-permute-done | bytes 524320 | tf_op jit(solution)/shard_map/cond/branch_17_fun/ppermute | solution.py:358
  28.1 0.0 collective-permute-start.106
  28.1 1.5 %collective-permute-start.104 = (bf16[64,16,256]{2,1,0:T(8,128)(2,1)S(1)}, bf16[64,16,256]{2,1,0:T(8,128)(2,1)}, u32[]{:S(2)}, u32[]{:S(2)}) collective-permute-start(bf16[64,16,256]{2,1,0:T(8,128)(2,1)S(1)} %get-tuple-element.353), channel_id=1, source_target_pairs={{0,0},{1,2},{2,1},{3,3},{4,4},{5,6},{6,5},{7,7},{8,8},{9,10},{10,9... | collective-permute-start | bytes 1572872 | tf_op jit(solution)/shard_map/cond/branch_17_fun/ppermute | solution.py:358
  29.5 0.0 collective-permute-start.105
  29.5 12.1 %collective-permute-done.106 = bf16[64,16,256]{2,1,0:T(8,128)(2,1)} collective-permute-done((bf16[64,16,256]{2,1,0:T(8,128)(2,1)}, bf16[64,16,256]{2,1,0:T(8,128)(2,1)}, u32[]{:S(2)}, u32[]{:S(2)}) %collective-permute-start.106) | collective-permute-done | bytes 524320 | tf_op jit(solution)/shard_map/cond/branch_17_fun/ppermute | solution.py:358
  41.6 0.0 collective-permute-start.107
  41.6 0.0 collective-permute-done.104
  41.6 0.0 collective-permute-done.105
  41.6 2.2 %collective-permute-done.107 = bf16[64,16,256]{2,1,0:T(8,128)(2,1)} collective-permute-done((bf16[64,16,256]{2,1,0:T(8,128)(2,1)}, bf16[64,16,256]{2,1,0:T(8,128)(2,1)}, u32[]{:S(2)}, u32[]{:S(2)}) %collective-permute-start.107) | collective-permute-done | bytes 524320 | tf_op jit(solution)/shard_map/cond/branch_17_fun/ppermute | solution.py:358
  43.9 0.0 copy-done.1
  43.9 9.1 %correlate.1 = (bf16[2,1024,128]{2,1,0:T(8,128)(2,1)S(1)}, bf16[2,1024,128]{2,1,0:T(8,128)(2,1)S(1)}) custom-call(s32[4]{0:T(128)S(1)} %copy-done.2, bf16[64,16,256]{2,1,0:T(8,128)(2,1)} %get-tuple-element.501.a1, bf16[64,16,256]{2,1,0:T(8,128)(2,1)} %get-tuple-element.502.a2, bf16[64,16,256]{2,1,0:T(8,128)(2,1)} %get-tuple-element.503.b1, ...), custom_call_target="tpu_custom_call" | custom-call | tf_op jit(solution)/shard_map/correlate/pallas_call | solution.py:176
  53.0 0.1 slice_bitcast_fusion
  53.1 20.9 %conditional.3 = (bf16[1024,128]{1,0:T(8,128)(2,1)}, bf16[1024,128]{1,0:T(8,128)(2,1)S(1)}, bf16[1024,128]{1,0:T(8,128)(2,1)}, bf16[1024,128]{1,0:T(8,128)(2,1)S...) conditional(s32[]{:T(128)} %bitcast, ...), branch_computations={%region_24.0_spmd, %region_25.0_spmd, %region_26.0_spmd, %region_2... | conditional | bytes 6291704 | solution.py:447
  53.2 1.4 %collective-permute-start.215 = (bf16[1024,128]{1,0:T(8,128)(2,1)S(1)}, bf16[1024,128]{1,0:T(8,128)(2,1)}, u32[]{:S(2)}, u32[]{:S(2)}) collective-permute-start(bf16[1024,128]{1,0:T(8,128)(2,1)S(1)} %get-tuple-element.449), channel_id=1, source_target_pairs={{0,0},{1,2},{2,1},{3,3},{4,4},{5,6},{6,5},{7,7},{8,8},{9,10},{10,9... | collective-permute-start | bytes 786440 | tf_op jit(solution)/shard_map/cond/branch_17_fun/ppermute | solution.py:358
  54.5 1.5 %collective-permute-start.216 = (bf16[1024,128]{1,0:T(8,128)(2,1)S(1)}, bf16[1024,128]{1,0:T(8,128)(2,1)}, u32[]{:S(2)}, u32[]{:S(2)}) collective-permute-start(bf16[1024,128]{1,0:T(8,128)(2,1)S(1)} %get-tuple-element.450), channel_id=1, source_target_pairs={{0,24},{1,25},{2,26},{3,27},{4,28},{5,29},{6,30},{7,31},{8,16},{9,... | collective-permute-start | bytes 786440 | tf_op jit(solution)/shard_map/cond/branch_17_fun/ppermute | solution.py:358
  56.1 2.7 %collective-permute-start.214 = (bf16[1024,128]{1,0:T(8,128)(2,1)S(1)}, bf16[1024,128]{1,0:T(8,128)(2,1)S(1)}, u32[]{:S(2)}, u32[]{:S(2)}) collective-permute-start(bf16[1024,128]{1,0:T(8,128)(2,1)S(1)} %get-tuple-element.448), channel_id=1, source_target_pairs={{0,1},{1,0},{2,3},{3,2},{4,5},{5,4},{6,7},{7,6},{8,9},{9,8},{10,11... | collective-permute-start | bytes 786440 | tf_op jit(solution)/shard_map/cond/branch_17_fun/ppermute | solution.py:358
  58.8 0.0 collective-permute-done.215
  58.8 4.2 %collective-permute-done.216 = bf16[1024,128]{1,0:T(8,128)(2,1)} collective-permute-done((bf16[1024,128]{1,0:T(8,128)(2,1)S(1)}, bf16[1024,128]{1,0:T(8,128)(2,1)}, u32[]{:S(2)}, u32[]{:S(2)}) %collective-permute-start.216) | collective-permute-done | bytes 262176 | tf_op jit(solution)/shard_map/cond/branch_17_fun/ppermute | solution.py:358
  63.0 1.9 %collective-permute-done.214 = bf16[1024,128]{1,0:T(8,128)(2,1)S(1)} collective-permute-done((bf16[1024,128]{1,0:T(8,128)(2,1)S(1)}, bf16[1024,128]{1,0:T(8,128)(2,1)S(1)}, u32[]{:S(2)}, u32[]{:S(2)}) %collective-permute-start.214) | collective-permute-done | bytes 262176 | tf_op jit(solution)/shard_map/cond/branch_17_fun/ppermute | solution.py:358
  64.8 1.7 %collective-permute-start.217 = (bf16[1024,128]{1,0:T(8,128)(2,1)S(1)}, bf16[1024,128]{1,0:T(8,128)(2,1)}, u32[]{:S(2)}, u32[]{:S(2)}) collective-permute-start(bf16[1024,128]{1,0:T(8,128)(2,1)S(1)} %get-tuple-element.451), channel_id=1, source_target_pairs={{0,1},{1,3},{2,0},{3,2},{4,5},{5,7},{6,4},{7,6},{8,9},{9,11},{10,8... | collective-permute-start | bytes 786440 | tf_op jit(solution)/shard_map/cond/branch_17_fun/ppermute | solution.py:358
  66.6 1.4 %collective-permute-start.218 = (bf16[1024,128]{1,0:T(8,128)(2,1)S(1)}, bf16[1024,128]{1,0:T(8,128)(2,1)}, u32[]{:S(2)}, u32[]{:S(2)}) collective-permute-start(bf16[1024,128]{1,0:T(8,128)(2,1)S(1)} %collective-permute-done.214), channel_id=1, source_target_pairs={{0,24},{1,25},{2,26},{3,27},{4,28},{5,29},{6,30},{7,31},{8,16},{9,... | collective-permute-start | bytes 786440 | tf_op jit(solution)/shard_map/cond/branch_17_fun/ppermute | solution.py:358
  68.0 0.9 %copy.253 = bf16[1024,128]{1,0:T(8,128)(2,1)S(1)} copy(bf16[1024,128]{1,0:T(8,128)(2,1)} %collective-permute-done.215) | data formatting | bytes 524288 | tf_op jit(solution)/shard_map/cond
  69.0 4.1 %collective-permute-done.217 = bf16[1024,128]{1,0:T(8,128)(2,1)} collective-permute-done((bf16[1024,128]{1,0:T(8,128)(2,1)S(1)}, bf16[1024,128]{1,0:T(8,128)(2,1)}, u32[]{:S(2)}, u32[]{:S(2)}) %collective-permute-start.217) | collective-permute-done | bytes 262176 | tf_op jit(solution)/shard_map/cond/branch_17_fun/ppermute | solution.py:358
  73.1 1.0 %copy.251 = bf16[1024,128]{1,0:T(8,128)(2,1)S(1)} copy(bf16[1024,128]{1,0:T(8,128)(2,1)} %collective-permute-done.217) | data formatting | bytes 524288 | tf_op jit(solution)/shard_map/cond
  74.0 0.0 collective-permute-done.218
  74.0 1.1 %maximum_select_fusion = bf16[2,1024,128]{2,1,0:T(8,128)(2,1)S(1)} fusion(bf16[1,1024,128]{2,1,0:T(8,128)(2,1)} %bitcast.7, bf16[1,1024,128]{2,1,0:T(8,128)(2,1)} %bitcast.6, bf16[1,1024,128]{2,1,0:T(8,128)(2,1)S(1)} %bitcast.15, bf16[1,1024,128]{2,1,0:T(8,128)(2,1)S(1)} %bitcast.14, pred[]{:T(512)} %bitcast.5), kind=kLoop, calls=%fused_computation | loop fusion | flops 786432 | bytes 1572865 | tf_op jit(solution)/shard_map/jit(_where)/select_n | solution.py:451
  75.1 0.1 collective-permute-start.248
  75.2 1.9 %collective-permute-done.248.got_ref = bf16[2,1024,128]{2,1,0:T(8,128)(2,1)S(1)} collective-permute-done((bf16[2,1024,128]{2,1,0:T(8,128)(2,1)S(1)}, bf16[2,1024,128]{2,1,0:T(8,128)(2,1)S(1)}, u32[]{:S(2)}, u32[]{:S(2)}) %collective-permute-start.248) | collective-permute-done | bytes 524320 | tf_op jit(solution)/shard_map/ppermute | solution.py:358
  77.1 2.1 %assemble.1 = bf16[32,128,128]{2,1,0:T(8,128)(2,1)} custom-call(s32[4]{0:T(128)S(1)} %copy-done.2, bf16[1024,128]{1,0:T(8,128)(2,1)S(1)} %get-tuple-element.518.far_ref, bf16[1024,128]{1,0:T(8,128)(2,1)S(1)} %get-tuple-element.520.near_ref, bf16[1024,128]{1,0:T(8,128)(2,1)} %get-tuple-element.521.here_ref, bf16[1024,128]{1,0:T(8,128)(2,1)} %get-tuple-element.522.there_ref, ...), custom_call_target="tpu_custom_call" | custom-call | tf_op jit(solution)/shard_map/assemble/pallas_call | solution.py:343
Async XLA Ops:
  0.0 7.4 %collective-permute-start.247 = (bf16[32,8,2048]{2,1,0:T(8,128)(2,1)}, bf16[32,8,2048]{2,1,0:T(8,128)(2,1)S(1)}, u32[]{:S(2)}, u32[]{:S(2)}) collective-permute-start(bf16[32,8,2048]{2,1,0:T(8,128)(2,1)} %raw_ref.1), channel_id=1, source_target_pairs={{0,4},{1,5},{2,6},{3,7},{4,0},{5,1},{6,2},{7,3},{8,12},{9,13},{10,... | collective-permute-start | bytes 3145736 | tf_op jit(solution)/shard_map/ppermute | solution.py:358
  1.8 0.6 copy-start.2
  2.4 1.2 %copy-start = (bf16[32,8,2048]{2,1,0:T(8,128)(2,1)S(1)}, bf16[32,8,2048]{2,1,0:T(8,128)(2,1)}, u32[]{:S(2)}) copy-start(bf16[32,8,2048]{2,1,0:T(8,128)(2,1)} %raw_ref.1) | copy-start | bytes 3145732
  7.3 36.5 %copy-start.1 = (bf16[256,1024]{1,0:T(8,128)(2,1)S(1)}, bf16[256,1024]{1,0:T(8,128)(2,1)}, u32[]{:S(2)}) copy-start(bf16[256,1024]{1,0:T(8,128)(2,1)} %constant.11.clone.table_ref) | copy-start | bytes 1572868
  9.4 15.5 %collective-permute-start.102 = (bf16[64,16,256]{2,1,0:T(8,128)(2,1)S(1)}, bf16[64,16,256]{2,1,0:T(8,128)(2,1)}, u32[]{:S(2)}, u32[]{:S(2)}) collective-permute-start(bf16[64,16,256]{2,1,0:T(8,128)(2,1)S(1)} %get-tuple-element.353), channel_id=1, source_target_pairs={{0,2},{1,0},{2,3},{3,1},{4,6},{5,4},{6,7},{7,5},{8,10},{9,8},{10,1... | collective-permute-start | bytes 1572872 | tf_op jit(solution)/shard_map/cond/branch_17_fun/ppermute | solution.py:358
  13.0 15.1 %collective-permute-start.103 = (bf16[64,16,256]{2,1,0:T(8,128)(2,1)S(1)}, bf16[64,16,256]{2,1,0:T(8,128)(2,1)}, u32[]{:S(2)}, u32[]{:S(2)}) collective-permute-start(bf16[64,16,256]{2,1,0:T(8,128)(2,1)S(1)} %get-tuple-element.352), channel_id=1, source_target_pairs={{0,16},{1,17},{2,18},{3,19},{4,20},{5,21},{6,22},{7,23},{8,24},{9,... | collective-permute-start | bytes 1572872 | tf_op jit(solution)/shard_map/cond/branch_17_fun/ppermute | solution.py:358
  28.1 13.6 %collective-permute-start.106 = (bf16[64,16,256]{2,1,0:T(8,128)(2,1)}, bf16[64,16,256]{2,1,0:T(8,128)(2,1)}, u32[]{:S(2)}, u32[]{:S(2)}) collective-permute-start(bf16[64,16,256]{2,1,0:T(8,128)(2,1)} %collective-permute-done.103), channel_id=1, source_target_pairs={{0,1},{1,0},{2,3},{3,2},{4,5},{5,4},{6,7},{7,6},{8,9},{9,8},{10,11... | collective-permute-start | bytes 1572872 | tf_op jit(solution)/shard_map/cond/branch_17_fun/ppermute | solution.py:358
  28.1 13.6 %collective-permute-start.104 = (bf16[64,16,256]{2,1,0:T(8,128)(2,1)S(1)}, bf16[64,16,256]{2,1,0:T(8,128)(2,1)}, u32[]{:S(2)}, u32[]{:S(2)}) collective-permute-start(bf16[64,16,256]{2,1,0:T(8,128)(2,1)S(1)} %get-tuple-element.353), channel_id=1, source_target_pairs={{0,0},{1,2},{2,1},{3,3},{4,4},{5,6},{6,5},{7,7},{8,8},{9,10},{10,9... | collective-permute-start | bytes 1572872 | tf_op jit(solution)/shard_map/cond/branch_17_fun/ppermute | solution.py:358
  29.5 12.1 %collective-permute-start.105 = (bf16[64,16,256]{2,1,0:T(8,128)(2,1)}, bf16[64,16,256]{2,1,0:T(8,128)(2,1)}, u32[]{:S(2)}, u32[]{:S(2)}) collective-permute-start(bf16[64,16,256]{2,1,0:T(8,128)(2,1)} %collective-permute-done.103), channel_id=1, source_target_pairs={{0,4},{1,5},{2,6},{3,7},{4,0},{5,1},{6,2},{7,3},{8,12},{9,13},{10,... | collective-permute-start | bytes 1572872 | tf_op jit(solution)/shard_map/cond/branch_17_fun/ppermute | solution.py:358
  41.6 2.3 %collective-permute-start.107 = (bf16[64,16,256]{2,1,0:T(8,128)(2,1)}, bf16[64,16,256]{2,1,0:T(8,128)(2,1)}, u32[]{:S(2)}, u32[]{:S(2)}) collective-permute-start(bf16[64,16,256]{2,1,0:T(8,128)(2,1)} %collective-permute-done.106), channel_id=1, source_target_pairs={{0,4},{1,5},{2,6},{3,7},{4,0},{5,1},{6,2},{7,3},{8,12},{9,13},{10,... | collective-permute-start | bytes 1572872 | tf_op jit(solution)/shard_map/cond/branch_17_fun/ppermute | solution.py:358
  53.2 5.6 %collective-permute-start.215 = (bf16[1024,128]{1,0:T(8,128)(2,1)S(1)}, bf16[1024,128]{1,0:T(8,128)(2,1)}, u32[]{:S(2)}, u32[]{:S(2)}) collective-permute-start(bf16[1024,128]{1,0:T(8,128)(2,1)S(1)} %get-tuple-element.449), channel_id=1, source_target_pairs={{0,0},{1,2},{2,1},{3,3},{4,4},{5,6},{6,5},{7,7},{8,8},{9,10},{10,9... | collective-permute-start | bytes 786440 | tf_op jit(solution)/shard_map/cond/branch_17_fun/ppermute | solution.py:358
  54.5 8.4 %collective-permute-start.216 = (bf16[1024,128]{1,0:T(8,128)(2,1)S(1)}, bf16[1024,128]{1,0:T(8,128)(2,1)}, u32[]{:S(2)}, u32[]{:S(2)}) collective-permute-start(bf16[1024,128]{1,0:T(8,128)(2,1)S(1)} %get-tuple-element.450), channel_id=1, source_target_pairs={{0,24},{1,25},{2,26},{3,27},{4,28},{5,29},{6,30},{7,31},{8,16},{9,... | collective-permute-start | bytes 786440 | tf_op jit(solution)/shard_map/cond/branch_17_fun/ppermute | solution.py:358
  56.1 8.8 %collective-permute-start.214 = (bf16[1024,128]{1,0:T(8,128)(2,1)S(1)}, bf16[1024,128]{1,0:T(8,128)(2,1)S(1)}, u32[]{:S(2)}, u32[]{:S(2)}) collective-permute-start(bf16[1024,128]{1,0:T(8,128)(2,1)S(1)} %get-tuple-element.448), channel_id=1, source_target_pairs={{0,1},{1,0},{2,3},{3,2},{4,5},{5,4},{6,7},{7,6},{8,9},{9,8},{10,11... | collective-permute-start | bytes 786440 | tf_op jit(solution)/shard_map/cond/branch_17_fun/ppermute | solution.py:358
  64.8 8.2 %collective-permute-start.217 = (bf16[1024,128]{1,0:T(8,128)(2,1)S(1)}, bf16[1024,128]{1,0:T(8,128)(2,1)}, u32[]{:S(2)}, u32[]{:S(2)}) collective-permute-start(bf16[1024,128]{1,0:T(8,128)(2,1)S(1)} %get-tuple-element.451), channel_id=1, source_target_pairs={{0,1},{1,3},{2,0},{3,2},{4,5},{5,7},{6,4},{7,6},{8,9},{9,11},{10,8... | collective-permute-start | bytes 786440 | tf_op jit(solution)/shard_map/cond/branch_17_fun/ppermute | solution.py:358
  66.6 7.4 %collective-permute-start.218 = (bf16[1024,128]{1,0:T(8,128)(2,1)S(1)}, bf16[1024,128]{1,0:T(8,128)(2,1)}, u32[]{:S(2)}, u32[]{:S(2)}) collective-permute-start(bf16[1024,128]{1,0:T(8,128)(2,1)S(1)} %collective-permute-done.214), channel_id=1, source_target_pairs={{0,24},{1,25},{2,26},{3,27},{4,28},{5,29},{6,30},{7,31},{8,16},{9,... | collective-permute-start | bytes 786440 | tf_op jit(solution)/shard_map/cond/branch_17_fun/ppermute | solution.py:358
  75.1 2.0 %collective-permute-start.248 = (bf16[2,1024,128]{2,1,0:T(8,128)(2,1)S(1)}, bf16[2,1024,128]{2,1,0:T(8,128)(2,1)S(1)}, u32[]{:S(2)}, u32[]{:S(2)}) collective-permute-start(bf16[2,1024,128]{2,1,0:T(8,128)(2,1)S(1)} %maximum_select_fusion), channel_id=1, source_target_pairs={{0,4},{1,5},{2,6},{3,7},{4,0},{5,1},{6,2},{7,3},{8,12},{9,13},{10,... | collective-permute-start | bytes 1572872 | tf_op jit(solution)/shard_map/ppermute | solution.py:358
